TPU v7x, 256 devices: a whole 4x4x8 slice. The times are simulated.
256 devices in a mesh: blk: 32 (over z, x_lo, core), narrow: 8 (over x_hi, y).
Axes of the slice: x: 4 (x_hi: 2, x_lo: 2; x = x_hi * 2 + x_lo), y: 4, z: 8, core: 2. Of those that a mesh axis runs over, the one named last changes fastest.
Arguments:
- tensor: float32 [448, 128, 4224], P('blk', 'narrow'), may hold values from -25 to 25
- factor_two: float32 [128, 64], replicated, may hold values from -0.5 to 0.5
- factor_three: float32 [16, 16], replicated, may hold values from -1.5 to 1.5
- factor_four: float32 [33, 16], replicated, may hold values from -1 to 1
- factor_five: float32 [8, 8], replicated, may hold values from -2 to 2
Outputs:
- gram_matrix: float32 [448, 448], P('blk', 'narrow')
All inputs are finite; a program needn't handle non-finite values.
Results may differ from a plain program's by a relative error of at most 0.0003.
Values may be sent and summed in bfloat16 or wider, within the bound.
No kernel may reach another device: no remote copies, remote signals or barrier semaphores. Data moves between devices by JAX's collectives and lax.ppermute only.
A program may use at most 128 MiB of HBM per device.

v0:
```python
import math

import jax
import jax.numpy as jnp
from jax import lax
from jax.sharding import PartitionSpec as P


def squeeze_cells(slab_rows, factor_three, factor_four, factor_five):
    row_count, depth_rows, cell_count = slab_rows.shape
    third_size = factor_three.shape[0]
    third_rank = factor_three.shape[1]
    pair_factor = (factor_four[:, None, :, None] * factor_five[None, :, None, :]).reshape(
        factor_four.shape[0] * factor_five.shape[0], factor_four.shape[1] * factor_five.shape[1]
    )
    flat_cells = slab_rows.reshape(row_count * depth_rows * third_size, cell_count // third_size)
    inner_cells = jnp.dot(
        flat_cells, pair_factor, precision=lax.Precision.HIGHEST, preferred_element_type=jnp.float32
    )
    inner_cells = inner_cells.reshape(row_count * depth_rows, third_size, pair_factor.shape[1])
    outer_cells = jnp.einsum(
        "mac,ar->mrc", inner_cells, factor_three, precision=lax.Precision.HIGHEST
    )
    return outer_cells.reshape(row_count, depth_rows, third_rank * pair_factor.shape[1])


def pair_products(left_rows, right_rows):
    return lax.dot_general(
        left_rows, right_rows, (((1,), (1,)), ((), ())), preferred_element_type=jnp.float32
    )


def per_device(tensor, factor_two, factor_three, factor_four, factor_five):
    row_count, depth_rows = (tensor.shape[0], tensor.shape[1])
    reduced = squeeze_cells(tensor, factor_three, factor_four, factor_five)
    first_row = lax.axis_index("narrow") * depth_rows
    factor_rows = lax.dynamic_slice_in_dim(factor_two, first_row, depth_rows, 0)
    expanded = jnp.einsum("mjk,jr->mrk", reduced, factor_rows, precision=lax.Precision.HIGHEST)
    core_rows = lax.psum_scatter(expanded, "narrow", scatter_dimension=2, tiled=True)
    rounded = core_rows.astype(jnp.bfloat16).reshape(row_count, -1)
    gram_scale = 1.0 / math.sqrt(rounded.shape[1] * lax.axis_size("narrow"))
    partial_value = pair_products(rounded, lax.all_gather(rounded, "blk", axis=0, tiled=True))
    gram_block = lax.psum_scatter(partial_value, "narrow", scatter_dimension=1, tiled=True)
    return gram_block * gram_scale


def solution(mesh):
    return jax.shard_map(
        per_device,
        mesh=mesh,
        in_specs=(P("blk", "narrow", None), P(), P(), P(), P()),
        out_specs=P("blk", "narrow"),
        check_vma=False,
    )
```

profile of v0, /device:TPU:6, one launch (start us, length us, event | category | flops | bytes accessed | tf_op | source)
XLA Modules:
  0.0 325.2 jit_solution(4109792219536564611)
XLA Ops:
  6.5 0.0 copy-start
  6.5 0.0 reduce-scatter.3.cloned.1.call-start
  6.5 0.0 copy-start.2
  6.5 6.6 %reshape.27 = f32[3584,264]{1,0:T(8,128)} reshape(f32[14,16,4224]{2,1,0:T(8,128)} %param.5) | data formatting | bytes 7569408 | tf_op jit(solution)/shard_map/reshape | solution.py:16
  13.2 0.0 copy-done.2
  13.2 0.1 copy.15
  13.2 0.0 copy-done.3
  13.3 0.2 broadcast_multiply_fusion
  13.5 1.1 mul.36
  14.5 9.6 %convolution_bitcast_fusion = f32[3584,128]{0,1:T(8,128)} fusion(f32[264,128]{1,0:T(8,128)S(1)} %mul.36, f32[3584,264]{1,0:T(8,128)} %reshape.27), kind=kOutput, calls=%fused_computation | convolution fusion | flops 1453326336 | bytes 5754880 | tf_op jit(solution)/shard_map/dot_general | solution.py:17
  24.1 0.0 copy-start.1
  24.1 1.8 copy.16
  25.9 0.0 copy-done.1
  25.9 2.9 convolution_bitcast_fusion.2
  28.9 1.6 reshape.29
  30.5 0.0 copy-done
  30.5 8.0 %convolution_bitcast_fusion.1 = f32[14,64,2048]{2,1,0:T(8,128)} fusion(f32[14,16,2048]{2,1,0:T(8,128)S(1)} %reshape.29, f32[128,64]{0,1:T(8,128)S(1)} %copy-done, s32[]{:T(128)S(6)} %select_n.3), kind=kOutput, calls=%fused_computation.1 | convolution fusion | flops 352321536 | bytes 9207812 | tf_op jit(solution)/shard_map/mjk,jr->mrk/dot_general | solution.py:38
  38.4 0.0 reduce-scatter.3.cloned.1.call-update
  38.5 0.0 copy-start.4
  38.5 0.2 all-gather.3.cloned.1.call-start
  38.7 113.3 %reduce-scatter.3.cloned.1.call-done = f32[14,64,256]{2,1,0:T(8,128)} async-done(((f32[14,64,2048]{2,1,0:T(8,128)}), f32[14,64,256]{2,1,0:T(8,128)}) %reduce-scatter.3.cloned.1.call-update) | async-done | bytes 917520 | tf_op jit(solution)/shard_map/reduce_scatter | solution.py:39
  152.0 1.2 convert_element_type.3
  153.2 1.1 reshape.31
  154.4 0.0 all-gather.3.cloned.1.call-update
  154.4 0.0 copy-done.4
  154.4 0.6 dynamic-slice
  155.7 0.3 copy.23
  156.0 97.8 %all-gather.3.cloned.1.call-done = bf16[32,14,16384]{2,1,0:T(8,128)(2,1)} async-done(((bf16[1,14,16384]{2,1,0:T(8,128)(2,1)}), bf16[32,14,16384]{2,1,0:T(8,128)(2,1)}) %all-gather.3.cloned.1.call-update) | async-done | bytes 14680080 | tf_op jit(solution)/shard_map/all_gather | solution.py:42
  253.8 14.7 %reshape.32 = bf16[448,16384]{1,0:T(8,128)(2,1)} reshape(bf16[32,14,16384]{2,1,0:T(8,128)(2,1)} %all-gather.3.cloned.1.call-done) | data formatting | bytes 29360128
  268.5 9.0 %fusion.4 = f32[14,448]{1,0:T(8,128)S(1)} fusion(bf16[14,16384]{1,0:T(8,128)(2,1)S(1)} %bitcast.30, bf16[448,16384]{1,0:T(8,128)(2,1)} %reshape.32), kind=kOutput, calls=%fused_computation.9 | convolution fusion | flops 205520896 | bytes 15163904 | tf_op jit(solution)/shard_map/dot_general | solution.py:28
  277.6 40.2 %all-reduce = f32[14,448]{1,0:T(8,128)S(1)} all-reduce(f32[14,448]{1,0:T(8,128)S(1)} %fusion.4), channel_id=3, replica_groups=mesh['blk'=32,'narrow'=8] {'narrow'}, use_global_device_ids=true, to_apply=%region_1.0.clone | all-reduce | flops 6272 | bytes 50176
  317.7 0.7 dynamic-slice_multiply_fusion
  (2 shorter events, 0.0 us)
Async XLA Ops:
  6.5 23.9 %copy-start = (f32[128,64]{0,1:T(8,128)S(1)}, f32[128,64]{0,1:T(8,128)}, u32[]{:S(2)}) copy-start(f32[128,64]{0,1:T(8,128)} %param.6) | copy-start | bytes 98308
  6.5 145.5 %reduce-scatter.3.cloned.1.call-start = ((), (), s32[]{:S(2)}) async-start(), calls=%async_computation.1 | async-start | bytes 8257536 | tf_op jit(solution)/shard_map/reduce_scatter | solution.py:39
  6.5 6.6 %copy-start.2 = (f32[33,16]{0,1:T(8,128)S(1)}, f32[33,16]{0,1:T(8,128)}, u32[]{:S(2)}) copy-start(f32[33,16]{0,1:T(8,128)} %param.8) | copy-start | bytes 6340
  6.5 6.7 %copy-start.3 = (f32[8,8]{1,0:T(8,128)S(1)}, f32[8,8]{1,0:T(8,128)}, u32[]{:S(2)}) copy-start(f32[8,8]{1,0:T(8,128)} %param.9) | copy-start | bytes 772
  24.1 1.8 copy-start.1
  38.5 115.9 %copy-start.4 = (u32[256]{0:T(256)S(1)}, u32[256]{0:T(256)}, u32[]{:S(2)}) copy-start(u32[256]{0:T(256)} %constant.15) | copy-start | bytes 3076
  38.5 215.3 %all-gather.3.cloned.1.call-start = ((), (), s32[]{:S(2)}) async-start(), calls=%async_computation.2 | async-start | bytes 17301504 | tf_op jit(solution)/shard_map/all_gather | solution.py:42
Sparse Core Ops, SparseCore 0:
  38.6 113.3 reduce-scatter.2
  154.5 99.2 all-gather.2
where the time goes:
time: 328 us; the launch traced here: 325 us
  waiting for transfers between devices  211 us (64%)
  blocking collectives  40.2 us (12%)
  matrix products  29.5 us (9%)
  local copies, waits for them, and re-layouts  28 us (9%)
  between operations  14.1 us (4%)
    reduce_scatter x1, waiting for transfers between devices, per_device(): lax.psum_scatter(expanded, 'narrow', scatter_dimension=2, tiled=True)  113 us
    all_gather x1, waiting for transfers between devices, per_device(): lax.all_gather(rounded, 'blk', axis=0, tiled=True)  97.8 us
    unnamed x1, blocking collectives  40.2 us
    unnamed x16, local copies, waits for them, and re-layouts  16.9 us
    dot_general x1, matrix products, squeeze_cells(): jnp.dot(flat_cells, pair_factor, precision=lax.Precision.HIGHEST, preferr...  9.59 us
    dot_general x1, matrix products, pair_products(): lax.dot_general(left_rows, right_rows, (((1,), (1,)), ((), ())), preferre...  9.05 us
    dot_general x1, matrix products, per_device(): jnp.einsum('mjk,jr->mrk', reduced, factor_rows, precision=lax.Precision.H...  7.95 us
    reshape x1, local copies, waits for them, and re-layouts, squeeze_cells(): slab_rows.reshape(row_count * depth_rows * third_size, cell_count // thir...  6.61 us
  transfers between devices with their start and end apart: 2, of which 2 were waited for; matrix products, arithmetic and copies ran while one was open for 0% of the time, Pallas kernels for 0%

commit v1 on v0

v1 whole, which is shorter than its diff:
```python
import math

import jax
import jax.numpy as jnp
from jax import lax
from jax.experimental import pallas as pl
from jax.experimental.pallas import tpu as pltpu
from jax.sharding import Mesh, PartitionSpec as P

F32 = jnp.float32
BF16 = jnp.bfloat16
ROWS, DEPTH, I3, I4, I5 = 14, 16, 16, 33, 8
R2, R3, R4, R5 = 64, 16, 16, 8
CELLS = I3 * I4 * I5
INNER = I4 * I5
PAIR = R4 * R5
PAD = 16
ROWS_STEP = 2
Z, XL, CORE, XH, Y = 8, 2, 2, 2, 4
NARROW = XH * Y
GROUPS = Z * XL
VMEM_LIMIT = 32 * 1024 * 1024


def split(value):
    high = value.astype(BF16)
    return high, (value - high.astype(F32)).astype(BF16)


def dot(left, right):
    return lax.dot_general(left, right, (((1,), (0,)), ((), ())), preferred_element_type=F32)


def exact_dot(left, right, dims):
    return lax.dot_general(
        left, right, (dims, ((), ())), precision=lax.Precision.HIGHEST, preferred_element_type=F32
    )


def squeeze_kernel(t_ref, f3_ref, f4t_ref, f5_ref, out_ref, pair_hl, mix_h, mix_l):
    step = pl.program_id(0)

    @pl.when(step == 0)
    def _():
        lane = lax.broadcasted_iota(jnp.int32, (R4, PAIR), 1)
        row = lax.broadcasted_iota(jnp.int32, (R4, PAIR), 0)
        spread_four = (lane // R5 == row).astype(F32)
        lane = lax.broadcasted_iota(jnp.int32, (R5, PAIR), 1)
        row = lax.broadcasted_iota(jnp.int32, (R5, PAIR), 0)
        spread_five = (lane % R5 == row).astype(F32)
        four = exact_dot(f4t_ref[...], spread_four, ((0,), (0,)))
        five = exact_dot(f5_ref[...], spread_five, ((1,), (0,)))
        pair = (four[:, None, :] * five[None, :, :]).reshape(INNER, PAIR)
        high, low = split(pair)
        pair_hl[:, :PAIR] = high
        pair_hl[:, PAIR:] = low
        size = R3 * DEPTH
        a_row = lax.broadcasted_iota(jnp.int32, (size, I3), 0) // DEPTH
        a_col = lax.broadcasted_iota(jnp.int32, (size, I3), 1)
        pick = (a_row == a_col).astype(F32)
        rows = exact_dot(pick, f3_ref[...], ((1,), (1,)))
        full = exact_dot(rows, pick, ((1,), (1,)))
        same = (
            lax.broadcasted_iota(jnp.int32, (size, size), 0) % DEPTH
            == lax.broadcasted_iota(jnp.int32, (size, size), 1) % DEPTH
        )
        high, low = split(jnp.where(same, full, 0.0))
        mix_h[...] = high
        mix_l[...] = low

    for local in range(ROWS_STEP):
        high, low = split(t_ref[local])
        left_h = jnp.concatenate([high[:, a * INNER:(a + 1) * INNER] for a in range(I3)], axis=0)
        left_l = jnp.concatenate([low[:, a * INNER:(a + 1) * INNER] for a in range(I3)], axis=0)
        both = dot(left_h, pair_hl[...])
        inner = both[:, :PAIR] + (both[:, PAIR:] + dot(left_l, pair_hl[:, :PAIR]))
        inner_h, inner_l = split(inner)
        both = dot(mix_h[...], jnp.concatenate([inner_h, inner_l], axis=1))
        outer = both[:, :PAIR] + (both[:, PAIR:] + dot(mix_l[...], inner_h))
        out_ref[:, step * ROWS_STEP + local] = outer.reshape(NARROW, -1, PAIR).astype(out_ref.dtype)


def squeeze(tensor, f3, f4t, f5):
    size = R3 * DEPTH
    return pl.pallas_call(
        squeeze_kernel,
        grid=(ROWS // ROWS_STEP,),
        in_specs=[
            pl.BlockSpec((ROWS_STEP, DEPTH, CELLS), lambda s: (s, 0, 0)),
            pl.BlockSpec((I3, R3), lambda s: (0, 0)),
            pl.BlockSpec((R4, I4), lambda s: (0, 0)),
            pl.BlockSpec((I5, R5), lambda s: (0, 0)),
        ],
        out_specs=pl.BlockSpec((NARROW, ROWS, size // NARROW, PAIR), lambda s: (0, 0, 0, 0)),
        out_shape=jax.ShapeDtypeStruct((NARROW, ROWS, size // NARROW, PAIR), BF16),
        scratch_shapes=[
            pltpu.VMEM((INNER, 2 * PAIR), BF16),
            pltpu.VMEM((size, size), BF16),
            pltpu.VMEM((size, size), BF16),
        ],
        compiler_params=pltpu.CompilerParams(vmem_limit_bytes=VMEM_LIMIT),
    )(tensor, f3, f4t, f5)


def expand_kernel(x_ref, f2t_ref, out_ref, rows_ref):
    high, low = split(f2t_ref[...])
    left = jnp.concatenate([high, low], axis=0)
    width = 2 * PAIR
    for i in range(ROWS):
        piece = x_ref[:, i]
        right = jnp.concatenate(
            [piece[:, h * DEPTH:(h + 1) * DEPTH].reshape(NARROW * DEPTH, PAIR) for h in range(2)], axis=1
        )
        both = dot(left, right)
        core = both[:R2] + both[R2:]
        for h in range(2):
            rows_ref[h, pl.ds(i, R2, stride=PAD), :] = core[:, h * PAIR:(h + 1) * PAIR]
    keep = lax.broadcasted_iota(jnp.int32, (R2, PAD, PAIR), 1) < ROWS
    for h in range(2):
        block = jnp.where(keep, rows_ref[h].reshape(R2, PAD, PAIR), 0.0)
        out_ref[:, :, :, h * PAIR:(h + 1) * PAIR] = block.astype(BF16).reshape(GROUPS, -1, PAD, PAIR)


def expand(gathered, f2t):
    return pl.pallas_call(
        expand_kernel,
        out_shape=jax.ShapeDtypeStruct((GROUPS, R2 // GROUPS, PAD, 2 * PAIR), BF16),
        scratch_shapes=[pltpu.VMEM((2, R2 * PAD, PAIR), F32)],
        compiler_params=pltpu.CompilerParams(vmem_limit_bytes=VMEM_LIMIT),
    )(gathered, f2t)


def gram_kernel(x_ref, out_ref):
    own = lax.axis_index("core")
    total = None
    for q in range(R2 // GROUPS):
        left = x_ref[own, :, q].reshape(GROUPS * PAD, 2 * PAIR)
        right = jnp.concatenate(
            [x_ref[c, g, q] for g in range(GROUPS) for c in range(CORE)], axis=0
        )
        part = lax.dot_general(left, right, (((1,), (1,)), ((), ())), preferred_element_type=F32)
        total = part if total is None else total + part
    first = lax.broadcasted_iota(jnp.int32, (8, 128), 1) < 64
    for g in range(GROUPS):
        for n in range(0, NARROW, 2):
            top = total[g * PAD:g * PAD + 8, n * 64:n * 64 + 128]
            bottom = total[g * PAD + 8:(g + 1) * PAD, n * 64:n * 64 + 128]
            out_ref[g * NARROW + n] = jnp.where(first, top, pltpu.roll(bottom, 64, 1))
            out_ref[g * NARROW + n + 1] = jnp.where(first, pltpu.roll(top, 64, 1), bottom)


def gram(blocks):
    return pl.pallas_call(
        gram_kernel,
        out_shape=jax.ShapeDtypeStruct((GROUPS * NARROW, 8, 128), F32),
        compiler_params=pltpu.CompilerParams(vmem_limit_bytes=VMEM_LIMIT),
    )(blocks)


def finish_kernel(x_ref, out_ref):
    scale = 1.0 / math.sqrt(R2 * R3 * R4 * R5)
    total = jnp.sum(x_ref[...], axis=0) * scale
    rows = jnp.concatenate([total[:, :64], total[:, 64:]], axis=0)[:ROWS]
    out_ref[...] = jnp.concatenate([rows[:, g * PAD:g * PAD + ROWS] for g in range(4)], axis=1)


def finish(parts):
    return pl.pallas_call(
        finish_kernel,
        out_shape=jax.ShapeDtypeStruct((ROWS, 4 * ROWS), F32),
        compiler_params=pltpu.CompilerParams(vmem_limit_bytes=VMEM_LIMIT),
    )(parts)


def per_device(tensor, f2, f3, f4, f5):
    with jax.named_scope("squeeze"):
        reduced = squeeze(tensor, f3, f4.T, f5)
    with jax.named_scope("depth_exchange"):
        gathered = lax.all_to_all(reduced, ("x_hi", "y"), 0, 0, tiled=True)
    with jax.named_scope("expand"):
        core = expand(gathered, f2.T)
    with jax.named_scope("row_exchange"):
        rows = lax.all_to_all(core, ("z", "x_lo"), 0, 0, tiled=True)
    with jax.named_scope("core_gather"):
        both = lax.all_gather(rows, "core")
    with jax.named_scope("gram"):
        parts = gram(both)
    with jax.named_scope("gram_exchange"):
        parts = lax.all_to_all(parts, ("z", "x_lo", "x_hi", "y"), 0, 0, tiled=True)
    with jax.named_scope("finish"):
        return finish(parts)


def solution(mesh):
    fine = Mesh(
        mesh.devices.reshape(Z, XL, CORE, XH, Y), ("z", "x_lo", "core", "x_hi", "y")
    )
    blk, narrow = ("z", "x_lo", "core"), ("x_hi", "y")
    return jax.shard_map(
        per_device,
        mesh=fine,
        in_specs=(P(blk, narrow, None), P(), P(), P(), P()),
        out_specs=P(blk, narrow),
        check_vma=False,
    )
```

time: 328 us -> 117 us (0.36)
  waiting for transfers between devices: 211 us -> 11.7 us
  blocking collectives: 40.2 us -> 77.1 us
  matrix products: 29.5 us -> 0 us
  local copies, waits for them, and re-layouts: 28 us -> 5.38 us
  Pallas kernels: 0 us -> 9.11 us
    reduce_scatter x1 -> x0, waiting for transfers between devices: 113 us -> none  [per_device(): lax.psum_scatter(expanded, 'narrow', scatter_dimension=2, tiled=True)]
    all_gather x1, waiting for transfers between devices: 97.8 us -> 11.7 us  [per_device(): both = lax.all_gather(rows, 'core')]
    all_to_all x0 -> x3, blocking collectives: none -> 77.1 us  [the longest x1 33 us: per_device(): parts = lax.all_to_all(parts, ('z', 'x_lo', 'x_hi', 'y'), 0, 0, tiled=True)]
    unnamed x1 -> x0, blocking collectives: 40.2 us -> none
    dot_general x4 -> x0, matrix products: 29.5 us -> none  [the longest x1 9.59 us: squeeze_cells(): jnp.dot(flat_cells, pair_factor, precision=lax.Precision.HIGHEST, preferr...]
    unnamed x16 -> x12, local copies, waits for them, and re-layouts: 16.9 us -> 5.38 us
    pallas_call x0 -> x4, Pallas kernels: none -> 9.11 us  [the longest x1 7.1 us: squeeze(): pl.pallas_call(squeeze_kernel, grid=(ROWS // ROWS_STEP,), in_specs=[pl.Bl...]
    reshape x2 -> x0, local copies, waits for them, and re-layouts: 8.2 us -> none  [the longest x1 6.61 us: squeeze_cells(): slab_rows.reshape(row_count * depth_rows * third_size, cell_count // thir...]
  transfers between devices with their start and end apart: 2 -> 1, of which waited for: 2 -> 1; matrix products, arithmetic and copies ran while one was open for 0% -> 0% of each run, Pallas kernels for 0% -> 0%
where the time goes in v1:
time: 117 us
  blocking collectives  77.1 us (66%)
  between operations  13.4 us (11%)
  waiting for transfers between devices  11.7 us (10%)
  Pallas kernels  9.11 us (8%)
  local copies, waits for them, and re-layouts  5.38 us (5%)
    all_to_all x1, blocking collectives, per_device(): parts = lax.all_to_all(parts, ('z', 'x_lo', 'x_hi', 'y'), 0, 0, tiled=True)  33 us
    all_to_all x1, blocking collectives, per_device(): rows = lax.all_to_all(core, ('z', 'x_lo'), 0, 0, tiled=True)  23.9 us
    all_to_all x1, blocking collectives, per_device(): gathered = lax.all_to_all(reduced, ('x_hi', 'y'), 0, 0, tiled=True)  20.2 us
    all_gather x1, waiting for transfers between devices, per_device(): both = lax.all_gather(rows, 'core')  11.7 us
    pallas_call x1, Pallas kernels, squeeze(): pl.pallas_call(squeeze_kernel, grid=(ROWS // ROWS_STEP,), in_specs=[pl.Bl...  7.1 us
    unnamed x12, local copies, waits for them, and re-layouts  5.38 us
  transfers between devices with their start and end apart: 1, of which 1 were waited for; matrix products, arithmetic and copies ran while one was open for 0% of the time, Pallas kernels for 0%

profile of v1, /device:TPU:6, one launch (start us, length us, event | category | flops | bytes accessed | tf_op | source)
XLA Modules:
  0.0 116.7 jit_solution(4901896865760801691)
XLA Ops:
  6.5 0.0 all-gather.3.cloned.1.call-start
  6.5 0.0 copy-start
  6.5 2.1 %copy-done = f32[14,16,4224]{2,1,0:T(8,128)S(1)} copy-done((f32[14,16,4224]{2,1,0:T(8,128)S(1)}, f32[14,16,4224]{2,1,0:T(8,128)}, u32[]{:S(2)}) %copy-start) | copy-done | bytes 3784728
  8.6 0.0 copy-start.3
  8.6 0.7 copy-done.3
  9.3 0.0 copy-start.4
  9.3 0.7 copy-done.4
  10.0 0.0 copy-start.5
  10.0 0.7 copy-done.5
  10.7 0.0 copy-start.2
  10.7 7.1 %squeeze.1 = bf16[8,14,32,128]{3,2,1,0:T(8,128)(2,1)S(1)} custom-call(f32[14,16,4224]{2,1,0:T(8,128)S(1)} %copy-done, f32[16,16]{1,0:T(8,128)S(1)} %copy-done.3, f32[16,33]{1,0:T(8,128)S(1)} %bitcast.5, f32[8,8]{1,0:T(8,128)S(1)} %copy-done.5), custom_call_target="tpu_custom_call" | custom-call | tf_op jit(solution)/shard_map/squeeze/pallas_call | solution.py:85
  17.8 20.2 %all_to_all.15.x_ref = bf16[8,14,32,128]{3,2,1,0:T(8,128)(2,1)S(1)} all-to-all(bf16[8,14,32,128]{3,2,1,0:T(8,128)(2,1)S(1)} %squeeze.1), channel_id=1, replica_groups=mesh['z'=8,'x_lo'=2,'core'=2,'x_hi'=2,'y'=4] {'x_hi','y'}, dimensions={0} | all-to-all | bytes 1835008 | tf_op jit(solution)/shard_map/depth_exchange/all_to_all | solution.py:179
  38.0 0.0 copy-done.2
  38.0 0.5 expand.1
  38.5 23.9 %all_to_all.16 = bf16[16,4,16,256]{3,2,1,0:T(8,128)(2,1)} all-to-all(bf16[16,4,16,256]{3,2,1,0:T(8,128)(2,1)S(1)} %expand.1), channel_id=1, replica_groups=mesh['z'=8,'x_lo'=2,'core'=2,'x_hi'=2,'y'=4] {'z','x_lo'}, dimensions={0} | all-to-all | bytes 1048576 | tf_op jit(solution)/shard_map/row_exchange/all_to_all | solution.py:183
  62.4 0.0 all-gather.3.cloned.1.call-update
  62.4 11.7 %all-gather.3.cloned.1.call-done = bf16[32,4,16,256]{3,2,1,0:T(8,128)(2,1)} async-done(((bf16[16,4,16,256]{3,2,1,0:T(8,128)(2,1)}), bf16[32,4,16,256]{3,2,1,0:T(8,128)(2,1)}) %all-gather.3.cloned.1.call-update) | async-done | bytes 1048592 | tf_op jit(solution)/shard_map/core_gather/all_gather | solution.py:185
  74.1 0.0 copy-start.1
  74.1 1.2 %copy-done.1 = bf16[32,4,16,256]{3,2,1,0:T(8,128)(2,1)S(1)} copy-done((bf16[32,4,16,256]{3,2,1,0:T(8,128)(2,1)S(1)}, bf16[32,4,16,256]{3,2,1,0:T(8,128)(2,1)}, u32[]{:S(2)}) %copy-start.1) | copy-done | bytes 1048600
  75.3 0.6 gram.1
  75.9 33.0 %all_to_all.17.x_ref = f32[128,8,128]{2,1,0:T(8,128)S(1)} all-to-all(f32[128,8,128]{2,1,0:T(8,128)S(1)} %gram.1), channel_id=1, replica_groups=mesh['z'=8,'x_lo'=2,'core'=2,'x_hi'=2,'y'=4] {'z','x_lo','x_hi','y'}, dimensions={0} | all-to-all | bytes 1048576 | tf_op jit(solution)/shard_map/gram_exchange/all_to_all | solution.py:189
  109.0 0.9 finish.1
Async XLA Ops:
  6.5 67.6 %all-gather.3.cloned.1.call-start = ((), (), s32[]{:S(2)}) async-start(), calls=%async_computation.3 | async-start | bytes 1572864 | tf_op jit(solution)/shard_map/core_gather/all_gather | solution.py:185
  6.5 2.1 %copy-start = (f32[14,16,4224]{2,1,0:T(8,128)S(1)}, f32[14,16,4224]{2,1,0:T(8,128)}, u32[]{:S(2)}) copy-start(f32[14,16,4224]{2,1,0:T(8,128)} %t_ref.1) | copy-start | bytes 11354116
  8.6 0.7 copy-start.3
  9.3 0.7 copy-start.4
  10.0 0.7 copy-start.5
  10.7 27.3 %copy-start.2 = (f32[128,64]{0,1:T(8,128)S(1)}, f32[128,64]{0,1:T(8,128)}, u32[]{:S(2)}) copy-start(f32[128,64]{0,1:T(8,128)} %param.6) | copy-start | bytes 98308
  74.1 1.2 %copy-start.1 = (bf16[32,4,16,256]{3,2,1,0:T(8,128)(2,1)S(1)}, bf16[32,4,16,256]{3,2,1,0:T(8,128)(2,1)}, u32[]{:S(2)}) copy-start(bf16[32,4,16,256]{3,2,1,0:T(8,128)(2,1)} %all-gather.3.cloned.1.call-done) | copy-start | bytes 3145732
Sparse Core Ops, SparseCore 0:
  62.5 11.5 all-gather.2

commit v2 on v1

--- a/solution.py
+++ b/solution.py
@@ -130,13 +130,12 @@
     )(gathered, f2t)
 
 
-def gram_kernel(x_ref, out_ref):
-    own = lax.axis_index("core")
+def gram_kernel(own_ref, other_ref, out_ref):
     total = None
     for q in range(R2 // GROUPS):
-        left = x_ref[own, :, q].reshape(GROUPS * PAD, 2 * PAIR)
+        left = own_ref[:, q].reshape(GROUPS * PAD, 2 * PAIR)
         right = jnp.concatenate(
-            [x_ref[c, g, q] for g in range(GROUPS) for c in range(CORE)], axis=0
+            [ref[g, q] for g in range(GROUPS) for ref in (own_ref, other_ref)], axis=0
         )
         part = lax.dot_general(left, right, (((1,), (1,)), ((), ())), preferred_element_type=F32)
         total = part if total is None else total + part
@@ -149,19 +148,23 @@
             out_ref[g * NARROW + n + 1] = jnp.where(first, pltpu.roll(top, 64, 1), bottom)
 
 
-def gram(blocks):
+def gram(own, other):
     return pl.pallas_call(
         gram_kernel,
         out_shape=jax.ShapeDtypeStruct((GROUPS * NARROW, 8, 128), F32),
         compiler_params=pltpu.CompilerParams(vmem_limit_bytes=VMEM_LIMIT),
-    )(blocks)
+    )(own, other)
 
 
 def finish_kernel(x_ref, out_ref):
     scale = 1.0 / math.sqrt(R2 * R3 * R4 * R5)
     total = jnp.sum(x_ref[...], axis=0) * scale
     rows = jnp.concatenate([total[:, :64], total[:, 64:]], axis=0)[:ROWS]
-    out_ref[...] = jnp.concatenate([rows[:, g * PAD:g * PAD + ROWS] for g in range(4)], axis=1)
+    group = [rows[:, g * PAD:g * PAD + ROWS] for g in range(4)]
+    first = lax.axis_index("core") == 0
+    out_ref[...] = jnp.where(
+        first, jnp.concatenate(group, axis=1), jnp.concatenate([group[g ^ 1] for g in range(4)], axis=1)
+    )
 
 
 def finish(parts):
@@ -181,10 +184,10 @@
         core = expand(gathered, f2.T)
     with jax.named_scope("row_exchange"):
         rows = lax.all_to_all(core, ("z", "x_lo"), 0, 0, tiled=True)
-    with jax.named_scope("core_gather"):
-        both = lax.all_gather(rows, "core")
+    with jax.named_scope("core_swap"):
+        other = lax.ppermute(rows, "core", [(0, 1), (1, 0)])
     with jax.named_scope("gram"):
-        parts = gram(both)
+        parts = gram(rows, other)
     with jax.named_scope("gram_exchange"):
         parts = lax.all_to_all(parts, ("z", "x_lo", "x_hi", "y"), 0, 0, tiled=True)
     with jax.named_scope("finish"):

time: 117 us -> 88.5 us (0.76)
  between operations: 13.4 us -> 0.03 us
  waiting for transfers between devices: 11.7 us -> 1.91 us
  blocking collectives: 77.1 us -> 72.6 us
  local copies, waits for them, and re-layouts: 5.38 us -> 4.15 us
    all_gather x1 -> x0, waiting for transfers between devices: 11.7 us -> none  [per_device(): both = lax.all_gather(rows, 'core')]
    all_to_all x1, blocking collectives: 33 us -> 28.7 us  [per_device(): parts = lax.all_to_all(parts, ('z', 'x_lo', 'x_hi', 'y'), 0, 0, tiled=True)]
    ppermute x0 -> x1, waiting for transfers between devices: none -> 1.91 us  [per_device(): other = lax.ppermute(rows, 'core', [(0, 1), (1, 0)])]
    unnamed x12 -> x10, local copies, waits for them, and re-layouts: 5.38 us -> 4.15 us
where the time goes in v2:
time: 88.5 us; the launch traced here: 87.8 us
  blocking collectives  72.6 us (82%)
  Pallas kernels  9.12 us (10%)
  local copies, waits for them, and re-layouts  4.15 us (5%)
  waiting for transfers between devices  1.91 us (2%)
    all_to_all x1, blocking collectives, per_device(): parts = lax.all_to_all(parts, ('z', 'x_lo', 'x_hi', 'y'), 0, 0, tiled=True)  28.7 us
    all_to_all x1, blocking collectives, per_device(): rows = lax.all_to_all(core, ('z', 'x_lo'), 0, 0, tiled=True)  23.8 us
    all_to_all x1, blocking collectives, per_device(): gathered = lax.all_to_all(reduced, ('x_hi', 'y'), 0, 0, tiled=True)  20.2 us
    pallas_call x1, Pallas kernels, squeeze(): pl.pallas_call(squeeze_kernel, grid=(ROWS // ROWS_STEP,), in_specs=[pl.Bl...  7.1 us
    unnamed x10, local copies, waits for them, and re-layouts  4.15 us
    ppermute x1, waiting for transfers between devices, per_device(): other = lax.ppermute(rows, 'core', [(0, 1), (1, 0)])  1.91 us
  transfers between devices with their start and end apart: 1, of which 1 were waited for; matrix products, arithmetic and copies ran while one was open for 0% of the time, Pallas kernels for 0%

profile of v2, /device:TPU:6, one launch (start us, length us, event | category | flops | bytes accessed | tf_op | source)
XLA Modules:
  0.0 87.8 jit_solution(15893417274467043703)
XLA Ops:
  0.0 0.0 copy-start
  0.0 2.1 %copy-done = f32[14,16,4224]{2,1,0:T(8,128)S(1)} copy-done((f32[14,16,4224]{2,1,0:T(8,128)S(1)}, f32[14,16,4224]{2,1,0:T(8,128)}, u32[]{:S(2)}) %copy-start) | copy-done | bytes 3784728
  2.1 0.0 copy-start.2
  2.1 0.7 copy-done.2
  2.8 0.0 copy-start.3
  2.8 0.7 copy-done.3
  3.5 0.0 copy-start.4
  3.5 0.7 copy-done.4
  4.2 0.0 copy-start.1
  4.2 7.1 %squeeze.1 = bf16[8,14,32,128]{3,2,1,0:T(8,128)(2,1)S(1)} custom-call(f32[14,16,4224]{2,1,0:T(8,128)S(1)} %copy-done, f32[16,16]{1,0:T(8,128)S(1)} %copy-done.2, f32[16,33]{1,0:T(8,128)S(1)} %bitcast.3, f32[8,8]{1,0:T(8,128)S(1)} %copy-done.4), custom_call_target="tpu_custom_call" | custom-call | tf_op jit(solution)/shard_map/squeeze/pallas_call | solution.py:85
  11.3 20.2 %all_to_all.15.x_ref = bf16[8,14,32,128]{3,2,1,0:T(8,128)(2,1)S(1)} all-to-all(bf16[8,14,32,128]{3,2,1,0:T(8,128)(2,1)S(1)} %squeeze.1), channel_id=1, replica_groups=mesh['z'=8,'x_lo'=2,'core'=2,'x_hi'=2,'y'=4] {'x_hi','y'}, dimensions={0} | all-to-all | bytes 1835008 | tf_op jit(solution)/shard_map/depth_exchange/all_to_all | solution.py:182
  31.4 0.0 copy-done.1
  31.4 0.5 expand.1
  32.0 23.8 %all_to_all.16.own_ref = bf16[16,4,16,256]{3,2,1,0:T(8,128)(2,1)S(1)} all-to-all(bf16[16,4,16,256]{3,2,1,0:T(8,128)(2,1)S(1)} %expand.1), channel_id=1, replica_groups=mesh['z'=8,'x_lo'=2,'core'=2,'x_hi'=2,'y'=4] {'z','x_lo'}, dimensions={0} | all-to-all | bytes 1048576 | tf_op jit(solution)/shard_map/row_exchange/all_to_all | solution.py:186
  55.8 0.0 collective-permute-start
  55.8 1.9 %collective-permute-done.other_ref = bf16[16,4,16,256]{3,2,1,0:T(8,128)(2,1)S(1)} collective-permute-done((bf16[16,4,16,256]{3,2,1,0:T(8,128)(2,1)S(1)}, bf16[16,4,16,256]{3,2,1,0:T(8,128)(2,1)S(1)}, u32[]{:S(2)}, u32[]{:S(2)}) %collective-permute-start) | collective-permute-done | bytes 524320 | tf_op jit(solution)/shard_map/core_swap/ppermute | solution.py:188
  57.7 0.6 gram.1
  58.3 28.7 %all_to_all.17.x_ref = f32[128,8,128]{2,1,0:T(8,128)S(1)} all-to-all(f32[128,8,128]{2,1,0:T(8,128)S(1)} %gram.1), channel_id=1, replica_groups=mesh['z'=8,'x_lo'=2,'core'=2,'x_hi'=2,'y'=4] {'z','x_lo','x_hi','y'}, dimensions={0} | all-to-all | bytes 1048576 | tf_op jit(solution)/shard_map/gram_exchange/all_to_all | solution.py:192
  87.0 0.9 %finish.1 = f32[14,56]{1,0:T(8,128)} custom-call(f32[128,8,128]{2,1,0:T(8,128)S(1)} %all_to_all.17.x_ref), custom_call_target="tpu_custom_call" | custom-call | tf_op jit(solution)/shard_map/finish/pallas_call | solution.py:171
Async XLA Ops:
  0.0 2.1 %copy-start = (f32[14,16,4224]{2,1,0:T(8,128)S(1)}, f32[14,16,4224]{2,1,0:T(8,128)}, u32[]{:S(2)}) copy-start(f32[14,16,4224]{2,1,0:T(8,128)} %t_ref.1) | copy-start | bytes 11354116
  2.1 0.7 copy-start.2
  2.8 0.7 copy-start.3
  3.5 0.7 copy-start.4
  4.2 27.3 %copy-start.1 = (f32[128,64]{0,1:T(8,128)S(1)}, f32[128,64]{0,1:T(8,128)}, u32[]{:S(2)}) copy-start(f32[128,64]{0,1:T(8,128)} %param.6) | copy-start | bytes 98308
  55.8 1.9 %collective-permute-start = (bf16[16,4,16,256]{3,2,1,0:T(8,128)(2,1)S(1)}, bf16[16,4,16,256]{3,2,1,0:T(8,128)(2,1)S(1)}, u32[]{:S(2)}, u32[]{:S(2)}) collective-permute-start(bf16[16,4,16,256]{3,2,1,0:T(8,128)(2,1)S(1)} %all_to_all.16.own_ref), channel_id=1, source_target_pairs={{0,8},{8,0},{1,9},{9,1},{2,10},{10,2},{3,11},{11,3},{4,12},{12,4},... | collective-permute-start | bytes 1572872 | tf_op jit(solution)/shard_map/core_swap/ppermute | solution.py:188

commit v3 on v2

--- a/solution.py
+++ b/solution.py
@@ -14,6 +14,7 @@
 CELLS = I3 * I4 * I5
 INNER = I4 * I5
 PAIR = R4 * R5
+MAIN = 256
 PAD = 16
 ROWS_STEP = 2
 Z, XL, CORE, XH, Y = 8, 2, 2, 2, 4
@@ -37,68 +38,89 @@
     )
 
 
-def squeeze_kernel(t_ref, f3_ref, f4t_ref, f5_ref, out_ref, pair_hl, mix_h, mix_l):
-    step = pl.program_id(0)
-
-    @pl.when(step == 0)
-    def _():
-        lane = lax.broadcasted_iota(jnp.int32, (R4, PAIR), 1)
-        row = lax.broadcasted_iota(jnp.int32, (R4, PAIR), 0)
-        spread_four = (lane // R5 == row).astype(F32)
-        lane = lax.broadcasted_iota(jnp.int32, (R5, PAIR), 1)
-        row = lax.broadcasted_iota(jnp.int32, (R5, PAIR), 0)
-        spread_five = (lane % R5 == row).astype(F32)
-        four = exact_dot(f4t_ref[...], spread_four, ((0,), (0,)))
-        five = exact_dot(f5_ref[...], spread_five, ((1,), (0,)))
-        pair = (four[:, None, :] * five[None, :, :]).reshape(INNER, PAIR)
-        high, low = split(pair)
-        pair_hl[:, :PAIR] = high
-        pair_hl[:, PAIR:] = low
-        size = R3 * DEPTH
-        a_row = lax.broadcasted_iota(jnp.int32, (size, I3), 0) // DEPTH
-        a_col = lax.broadcasted_iota(jnp.int32, (size, I3), 1)
-        pick = (a_row == a_col).astype(F32)
-        rows = exact_dot(pick, f3_ref[...], ((1,), (1,)))
-        full = exact_dot(rows, pick, ((1,), (1,)))
-        same = (
-            lax.broadcasted_iota(jnp.int32, (size, size), 0) % DEPTH
-            == lax.broadcasted_iota(jnp.int32, (size, size), 1) % DEPTH
-        )
-        high, low = split(jnp.where(same, full, 0.0))
-        mix_h[...] = high
-        mix_l[...] = low
-
-    for local in range(ROWS_STEP):
-        high, low = split(t_ref[local])
-        left_h = jnp.concatenate([high[:, a * INNER:(a + 1) * INNER] for a in range(I3)], axis=0)
-        left_l = jnp.concatenate([low[:, a * INNER:(a + 1) * INNER] for a in range(I3)], axis=0)
-        both = dot(left_h, pair_hl[...])
-        inner = both[:, :PAIR] + (both[:, PAIR:] + dot(left_l, pair_hl[:, :PAIR]))
-        inner_h, inner_l = split(inner)
-        both = dot(mix_h[...], jnp.concatenate([inner_h, inner_l], axis=1))
-        outer = both[:, :PAIR] + (both[:, PAIR:] + dot(mix_l[...], inner_h))
-        out_ref[:, step * ROWS_STEP + local] = outer.reshape(NARROW, -1, PAIR).astype(out_ref.dtype)
+def squeeze_kernel(t_hbm, f3_hbm, f4t_hbm, f5_hbm, out_ref, t_ref, f3_ref, f4t_ref, f5_ref, main_h, main_l, rest, mix_h, mix_l, sems):
+    small = [
+        pltpu.make_async_copy(src, dst, sems.at[ROWS + n])
+        for n, (src, dst) in enumerate(((f3_hbm, f3_ref), (f4t_hbm, f4t_ref), (f5_hbm, f5_ref)))
+    ]
+    loads = [pltpu.make_async_copy(t_hbm.at[i], t_ref.at[i], sems.at[i]) for i in range(ROWS)]
+    for copy in small + loads:
+        copy.start()
+    for copy in small:
+        copy.wait()
+
+    lane = lax.broadcasted_iota(jnp.int32, (R4, PAIR), 1)
+    row = lax.broadcasted_iota(jnp.int32, (R4, PAIR), 0)
+    spread_four = (lane // R5 == row).astype(F32)
+    lane = lax.broadcasted_iota(jnp.int32, (R5, PAIR), 1)
+    row = lax.broadcasted_iota(jnp.int32, (R5, PAIR), 0)
+    spread_five = (lane % R5 == row).astype(F32)
+    four = exact_dot(f4t_ref[...], spread_four, ((0,), (0,)))
+    five = exact_dot(f5_ref[...], spread_five, ((1,), (0,)))
+    pair = (four[:, None, :] * five[None, :, :]).reshape(INNER, PAIR)
+    high, low = split(pair)
+    main_h[:, :PAIR] = high
+    main_h[:, PAIR:] = low
+    tail_h, tail_l = high[MAIN:], low[MAIN:]
+    rest[...] = jnp.concatenate(
+        [
+            jnp.concatenate([tail_h, tail_l], axis=1),
+            jnp.concatenate([tail_h, jnp.zeros_like(tail_l)], axis=1),
+        ],
+        axis=0,
+    )
+    size = R3 * DEPTH
+    a_row = lax.broadcasted_iota(jnp.int32, (size, I3), 0) // DEPTH
+    a_col = lax.broadcasted_iota(jnp.int32, (size, I3), 1)
+    pick = (a_row == a_col).astype(F32)
+    rows = exact_dot(pick, f3_ref[...], ((1,), (1,)))
+    full = exact_dot(rows, pick, ((1,), (1,)))
+    same = (
+        lax.broadcasted_iota(jnp.int32, (size, size), 0) % DEPTH
+        == lax.broadcasted_iota(jnp.int32, (size, size), 1) % DEPTH
+    )
+    high, low = split(jnp.where(same, full, 0.0))
+    mix_h[...] = high
+    mix_l[...] = low
+
+    size_in = R3 * DEPTH
+    for base in range(0, ROWS, 7):
+        group = range(base, base + 7)
+        for i in group:
+            loads[i].wait()
+        halves = [split(t_ref[i]) for i in group]
+        starts = [a * INNER for a in range(I3)]
+        left_h = jnp.concatenate([h[:, s:s + INNER] for h, _ in halves for s in starts], axis=0)
+        left_l = jnp.concatenate([l[:, s:s + INNER] for _, l in halves for s in starts], axis=0)
+        both = dot(left_h, main_h[...])
+        stack = both[:, :PAIR] + (both[:, PAIR:] + dot(left_l, main_h[:, :PAIR]))
+        for n, i in enumerate(group):
+            inner_h, inner_l = split(stack[n * size_in:(n + 1) * size_in])
+            both = dot(mix_h[...], jnp.concatenate([inner_h, inner_l], axis=1))
+            outer = both[:, :PAIR] + (both[:, PAIR:] + dot(mix_l[...], inner_h))
+            out_ref[:, i] = outer.reshape(NARROW, -1, PAIR).astype(out_ref.dtype)
 
 
 def squeeze(tensor, f3, f4t, f5):
     size = R3 * DEPTH
+    hbm = pl.BlockSpec(memory_space=pltpu.MemorySpace.HBM)
     return pl.pallas_call(
         squeeze_kernel,
-        grid=(ROWS // ROWS_STEP,),
-        in_specs=[
-            pl.BlockSpec((ROWS_STEP, DEPTH, CELLS), lambda s: (s, 0, 0)),
-            pl.BlockSpec((I3, R3), lambda s: (0, 0)),
-            pl.BlockSpec((R4, I4), lambda s: (0, 0)),
-            pl.BlockSpec((I5, R5), lambda s: (0, 0)),
-        ],
-        out_specs=pl.BlockSpec((NARROW, ROWS, size // NARROW, PAIR), lambda s: (0, 0, 0, 0)),
+        in_specs=[hbm] * 4,
         out_shape=jax.ShapeDtypeStruct((NARROW, ROWS, size // NARROW, PAIR), BF16),
         scratch_shapes=[
+            pltpu.VMEM((ROWS, DEPTH, CELLS), F32),
+            pltpu.VMEM((I3, R3), F32),
+            pltpu.VMEM((R4, I4), F32),
+            pltpu.VMEM((I5, R5), F32),
             pltpu.VMEM((INNER, 2 * PAIR), BF16),
+            pltpu.VMEM((MAIN, PAIR), BF16),
+            pltpu.VMEM((2 * (INNER - MAIN), 2 * PAIR), BF16),
             pltpu.VMEM((size, size), BF16),
             pltpu.VMEM((size, size), BF16),
+            pltpu.SemaphoreType.DMA((ROWS + 3,)),
         ],
-        compiler_params=pltpu.CompilerParams(vmem_limit_bytes=VMEM_LIMIT),
+        compiler_params=pltpu.CompilerParams(vmem_limit_bytes=61 * 1024 * 1024),
     )(tensor, f3, f4t, f5)
 
 

time: 88.5 us -> 83.3 us (0.941)
  local copies, waits for them, and re-layouts: 4.15 us -> 0.01 us
  Pallas kernels: 9.12 us -> 7.99 us
    unnamed x10 -> x2, local copies, waits for them, and re-layouts: 4.15 us -> 0.01 us
    pallas_call x1, Pallas kernels: 7.1 us -> 5.98 us  [squeeze(): pl.pallas_call(squeeze_kernel, in_specs=[hbm] * 4, out_shape=jax.ShapeDty...]
where the time goes in v3:
time: 83.3 us; the launch traced here: 82.8 us
  blocking collectives  72.8 us (87%)
  Pallas kernels  7.99 us (10%)
  waiting for transfers between devices  1.91 us (2%)
    all_to_all x1, blocking collectives, per_device(): parts = lax.all_to_all(parts, ('z', 'x_lo', 'x_hi', 'y'), 0, 0, tiled=True)  28.7 us
    all_to_all x1, blocking collectives, per_device(): rows = lax.all_to_all(core, ('z', 'x_lo'), 0, 0, tiled=True)  23.7 us
    all_to_all x1, blocking collectives, per_device(): gathered = lax.all_to_all(reduced, ('x_hi', 'y'), 0, 0, tiled=True)  20.4 us
    pallas_call x1, Pallas kernels, squeeze(): pl.pallas_call(squeeze_kernel, in_specs=[hbm] * 4, out_shape=jax.ShapeDty...  5.98 us
    ppermute x1, waiting for transfers between devices, per_device(): other = lax.ppermute(rows, 'core', [(0, 1), (1, 0)])  1.91 us
  transfers between devices with their start and end apart: 1, of which 1 were waited for; matrix products, arithmetic and copies ran while one was open for 0% of the time, Pallas kernels for 0%

profile of v3, /device:TPU:6, one launch (start us, length us, event | category | flops | bytes accessed | tf_op | source)
XLA Modules:
  0.0 82.8 jit_solution(6944325510751729499)
XLA Ops:
  0.0 0.0 copy-start
  0.0 6.0 %squeeze.1 = bf16[8,14,32,128]{3,2,1,0:T(8,128)(2,1)} custom-call(f32[14,16,4224]{2,1,0:T(8,128)} %t_hbm.1, f32[16,16]{1,0:T(8,128)} %f3_hbm.1, f32[16,33]{1,0:T(8,128)} %bitcast.3, f32[8,8]{1,0:T(8,128)} %f5_hbm.1), custom_call_target="tpu_custom_call" | custom-call | tf_op jit(solution)/shard_map/squeeze/pallas_call | solution.py:107
  6.0 20.4 %all_to_all.15.x_ref = bf16[8,14,32,128]{3,2,1,0:T(8,128)(2,1)S(1)} all-to-all(bf16[8,14,32,128]{3,2,1,0:T(8,128)(2,1)} %squeeze.1), channel_id=1, replica_groups=mesh['z'=8,'x_lo'=2,'core'=2,'x_hi'=2,'y'=4] {'x_hi','y'}, dimensions={0} | all-to-all | bytes 1835008 | tf_op jit(solution)/shard_map/depth_exchange/all_to_all | solution.py:204
  26.4 0.0 copy-done
  26.4 0.5 expand.1
  26.9 23.7 %all_to_all.16.own_ref = bf16[16,4,16,256]{3,2,1,0:T(8,128)(2,1)S(1)} all-to-all(bf16[16,4,16,256]{3,2,1,0:T(8,128)(2,1)S(1)} %expand.1), channel_id=1, replica_groups=mesh['z'=8,'x_lo'=2,'core'=2,'x_hi'=2,'y'=4] {'z','x_lo'}, dimensions={0} | all-to-all | bytes 1048576 | tf_op jit(solution)/shard_map/row_exchange/all_to_all | solution.py:208
  50.7 0.0 collective-permute-start
  50.7 1.9 %collective-permute-done.other_ref = bf16[16,4,16,256]{3,2,1,0:T(8,128)(2,1)S(1)} collective-permute-done((bf16[16,4,16,256]{3,2,1,0:T(8,128)(2,1)S(1)}, bf16[16,4,16,256]{3,2,1,0:T(8,128)(2,1)S(1)}, u32[]{:S(2)}, u32[]{:S(2)}) %collective-permute-start) | collective-permute-done | bytes 524320 | tf_op jit(solution)/shard_map/core_swap/ppermute | solution.py:210
  52.6 0.6 gram.1
  53.2 28.7 %all_to_all.17.x_ref = f32[128,8,128]{2,1,0:T(8,128)S(1)} all-to-all(f32[128,8,128]{2,1,0:T(8,128)S(1)} %gram.1), channel_id=1, replica_groups=mesh['z'=8,'x_lo'=2,'core'=2,'x_hi'=2,'y'=4] {'z','x_lo','x_hi','y'}, dimensions={0} | all-to-all | bytes 1048576 | tf_op jit(solution)/shard_map/gram_exchange/all_to_all | solution.py:214
  81.9 0.9 %finish.1 = f32[14,56]{1,0:T(8,128)} custom-call(f32[128,8,128]{2,1,0:T(8,128)S(1)} %all_to_all.17.x_ref), custom_call_target="tpu_custom_call" | custom-call | tf_op jit(solution)/shard_map/finish/pallas_call | solution.py:193
Async XLA Ops:
  0.0 26.4 %copy-start = (f32[128,64]{0,1:T(8,128)S(1)}, f32[128,64]{0,1:T(8,128)}, u32[]{:S(2)}) copy-start(f32[128,64]{0,1:T(8,128)} %param.6) | copy-start | bytes 98308
  50.7 1.9 %collective-permute-start = (bf16[16,4,16,256]{3,2,1,0:T(8,128)(2,1)S(1)}, bf16[16,4,16,256]{3,2,1,0:T(8,128)(2,1)S(1)}, u32[]{:S(2)}, u32[]{:S(2)}) collective-permute-start(bf16[16,4,16,256]{3,2,1,0:T(8,128)(2,1)S(1)} %all_to_all.16.own_ref), channel_id=1, source_target_pairs={{0,8},{8,0},{1,9},{9,1},{2,10},{10,2},{3,11},{11,3},{4,12},{12,4},... | collective-permute-start | bytes 1572872 | tf_op jit(solution)/shard_map/core_swap/ppermute | solution.py:210

commit v4 on v3

--- a/solution.py
+++ b/solution.py
@@ -9,12 +9,14 @@
 
 F32 = jnp.float32
 BF16 = jnp.bfloat16
+F16 = jnp.float16
 ROWS, DEPTH, I3, I4, I5 = 14, 16, 16, 33, 8
 R2, R3, R4, R5 = 64, 16, 16, 8
 CELLS = I3 * I4 * I5
 INNER = I4 * I5
 PAIR = R4 * R5
 MAIN = 256
+WIDE = R3 * DEPTH // 8
 PAD = 16
 ROWS_STEP = 2
 Z, XL, CORE, XH, Y = 8, 2, 2, 2, 4
@@ -30,6 +32,10 @@
 
 def dot(left, right):
     return lax.dot_general(left, right, (((1,), (0,)), ((), ())), preferred_element_type=F32)
+
+
+def exponent(peak):
+    return jnp.floor(jnp.log2(jnp.maximum(peak, 1e-30))) - 14.0
 
 
 def exact_dot(left, right, dims):
@@ -84,6 +90,7 @@
     mix_l[...] = low
 
     size_in = R3 * DEPTH
+    peak = jnp.zeros((8, PAIR), F32)
     for base in range(0, ROWS, 7):
         group = range(base, base + 7)
         for i in group:
@@ -98,7 +105,15 @@
             inner_h, inner_l = split(stack[n * size_in:(n + 1) * size_in])
             both = dot(mix_h[...], jnp.concatenate([inner_h, inner_l], axis=1))
             outer = both[:, :PAIR] + (both[:, PAIR:] + dot(mix_l[...], inner_h))
-            out_ref[:, i] = outer.reshape(NARROW, -1, PAIR).astype(out_ref.dtype)
+            out_ref[:, i * WIDE:(i + 1) * WIDE] = outer.reshape(NARROW, WIDE, PAIR)
+            peak = jnp.maximum(peak, jnp.max(jnp.abs(outer).reshape(-1, 8, PAIR), axis=0))
+
+    level = exponent(jnp.broadcast_to(jnp.max(peak, keepdims=True), (8, PAIR)))
+    factor = jnp.exp2(-level)
+    for n in range(NARROW):
+        block = out_ref[n, :ROWS * WIDE].reshape(-1, 8, PAIR) * factor
+        out_ref[n, :ROWS * WIDE] = block.reshape(ROWS * WIDE, PAIR)
+        out_ref[n, ROWS * WIDE:] = level
 
 
 def squeeze(tensor, f3, f4t, f5):
@@ -107,7 +122,7 @@
     return pl.pallas_call(
         squeeze_kernel,
         in_specs=[hbm] * 4,
-        out_shape=jax.ShapeDtypeStruct((NARROW, ROWS, size // NARROW, PAIR), BF16),
+        out_shape=jax.ShapeDtypeStruct((NARROW, ROWS * WIDE + 8, PAIR), F32),
         scratch_shapes=[
             pltpu.VMEM((ROWS, DEPTH, CELLS), F32),
             pltpu.VMEM((I3, R3), F32),
@@ -127,14 +142,18 @@
 def expand_kernel(x_ref, f2t_ref, out_ref, rows_ref):
     high, low = split(f2t_ref[...])
     left = jnp.concatenate([high, low], axis=0)
-    width = 2 * PAIR
+    factor = jnp.exp2(x_ref[:, ROWS * WIDE:])
     for i in range(ROWS):
-        piece = x_ref[:, i]
-        right = jnp.concatenate(
-            [piece[:, h * DEPTH:(h + 1) * DEPTH].reshape(NARROW * DEPTH, PAIR) for h in range(2)], axis=1
+        piece = x_ref[:, i * WIDE:(i + 1) * WIDE].reshape(NARROW, WIDE // 8, 8, PAIR) * factor[:, None]
+        piece_h, piece_l = split(piece.reshape(NARROW, WIDE, PAIR))
+        right_h, right_l = (
+            jnp.concatenate(
+                [p[:, h * DEPTH:(h + 1) * DEPTH].reshape(NARROW * DEPTH, PAIR) for h in range(2)], axis=1
+            )
+            for p in (piece_h, piece_l)
         )
-        both = dot(left, right)
-        core = both[:R2] + both[R2:]
+        both = dot(left, right_h)
+        core = both[:R2] + (both[R2:] + dot(high, right_l))
         for h in range(2):
             rows_ref[h, pl.ds(i, R2, stride=PAD), :] = core[:, h * PAIR:(h + 1) * PAIR]
     keep = lax.broadcasted_iota(jnp.int32, (R2, PAD, PAIR), 1) < ROWS
@@ -161,11 +180,15 @@
         )
         part = lax.dot_general(left, right, (((1,), (1,)), ((), ())), preferred_element_type=F32)
         total = part if total is None else total + part
+    peak = jnp.max(jnp.abs(total), axis=0, keepdims=True)
+    level = exponent(jnp.broadcast_to(jnp.max(peak, axis=1, keepdims=True), (8, 128)))
+    total = total * jnp.exp2(-level[:1, :1])
     first = lax.broadcasted_iota(jnp.int32, (8, 128), 1) < 64
+    last = lax.broadcasted_iota(jnp.int32, (8, 128), 0) == 7
     for g in range(GROUPS):
         for n in range(0, NARROW, 2):
             top = total[g * PAD:g * PAD + 8, n * 64:n * 64 + 128]
-            bottom = total[g * PAD + 8:(g + 1) * PAD, n * 64:n * 64 + 128]
+            bottom = jnp.where(last, level, total[g * PAD + 8:(g + 1) * PAD, n * 64:n * 64 + 128])
             out_ref[g * NARROW + n] = jnp.where(first, top, pltpu.roll(bottom, 64, 1))
             out_ref[g * NARROW + n + 1] = jnp.where(first, pltpu.roll(top, 64, 1), bottom)
 
@@ -180,7 +203,8 @@
 
 def finish_kernel(x_ref, out_ref):
     scale = 1.0 / math.sqrt(R2 * R3 * R4 * R5)
-    total = jnp.sum(x_ref[...], axis=0) * scale
+    factor = jnp.exp2(x_ref[:, 7:8, 64:65])
+    total = jnp.sum(x_ref[...] * factor, axis=0) * scale
     rows = jnp.concatenate([total[:, :64], total[:, 64:]], axis=0)[:ROWS]
     group = [rows[:, g * PAD:g * PAD + ROWS] for g in range(4)]
     first = lax.axis_index("core") == 0
@@ -197,11 +221,16 @@
     )(parts)
 
 
+def exchange(value, axes):
+    sent = lax.all_to_all(value.astype(F16), axes, 0, 0, tiled=True)
+    return sent.astype(F32)
+
+
 def per_device(tensor, f2, f3, f4, f5):
     with jax.named_scope("squeeze"):
         reduced = squeeze(tensor, f3, f4.T, f5)
     with jax.named_scope("depth_exchange"):
-        gathered = lax.all_to_all(reduced, ("x_hi", "y"), 0, 0, tiled=True)
+        gathered = exchange(reduced, ("x_hi", "y"))
     with jax.named_scope("expand"):
         core = expand(gathered, f2.T)
     with jax.named_scope("row_exchange"):
@@ -211,7 +240,7 @@
     with jax.named_scope("gram"):
         parts = gram(rows, other)
     with jax.named_scope("gram_exchange"):
-        parts = lax.all_to_all(parts, ("z", "x_lo", "x_hi", "y"), 0, 0, tiled=True)
+        parts = exchange(parts, ("z", "x_lo", "x_hi", "y"))
     with jax.named_scope("finish"):
         return finish(parts)
 

time: 83.3 us -> 81.6 us (0.980)
  blocking collectives: 72.8 us -> 67.7 us
  other arithmetic: 0 us -> 1.83 us
  Pallas kernels: 7.99 us -> 9.19 us
    all_to_all x2, blocking collectives: 49.1 us -> 43.8 us  [exchange(): sent = lax.all_to_all(value.astype(F16), axes, 0, 0, tiled=True)]
    convert_element_type x0 -> x4, other arithmetic: none -> 1.83 us  [the longest x2 1.67 us: exchange(): sent = lax.all_to_all(value.astype(F16), axes, 0, 0, tiled=True)]
where the time goes in v4:
time: 81.6 us; the launch traced here: 81.3 us
  blocking collectives  67.7 us (83%)
  Pallas kernels  9.19 us (11%)
  waiting for transfers between devices  1.91 us (2%)
  other arithmetic  1.83 us (2%)
    all_to_all x2, blocking collectives, exchange(): sent = lax.all_to_all(value.astype(F16), axes, 0, 0, tiled=True)  43.8 us
    all_to_all x1, blocking collectives, per_device(): rows = lax.all_to_all(core, ('z', 'x_lo'), 0, 0, tiled=True)  23.9 us
    pallas_call x1, Pallas kernels, squeeze(): pl.pallas_call(squeeze_kernel, in_specs=[hbm] * 4, out_shape=jax.ShapeDty...  6.57 us
    ppermute x1, waiting for transfers between devices, per_device(): other = lax.ppermute(rows, 'core', [(0, 1), (1, 0)])  1.91 us
    convert_element_type x2, other arithmetic, exchange(): sent = lax.all_to_all(value.astype(F16), axes, 0, 0, tiled=True)  1.67 us
  transfers between devices with their start and end apart: 1, of which 1 were waited for; matrix products, arithmetic and copies ran while one was open for 0% of the time, Pallas kernels for 0%

profile of v4, /device:TPU:6, one launch (start us, length us, event | category | flops | bytes accessed | tf_op | source)
XLA Modules:
  0.0 81.3 jit_solution(6784504729009271023)
XLA Ops:
  0.0 6.6 %squeeze.1 = f32[8,456,128]{2,1,0:T(8,128)} custom-call(f32[14,16,4224]{2,1,0:T(8,128)} %t_hbm.1, f32[16,16]{1,0:T(8,128)} %f3_hbm.1, f32[16,33]{1,0:T(8,128)} %bitcast.3, f32[8,8]{1,0:T(8,128)} %f5_hbm.1), custom_call_target="tpu_custom_call" | custom-call | tf_op jit(solution)/shard_map/squeeze/pallas_call | solution.py:122
  6.6 1.6 %convert_element_type.12 = f16[8,456,128]{2,1,0:T(8,128)(2,1)S(1)} convert(f32[8,456,128]{2,1,0:T(8,128)} %squeeze.1) | non-fusion elementwise | flops 466944 | bytes 2801664 | tf_op jit(solution)/shard_map/depth_exchange/convert_element_type | solution.py:225
  8.2 20.3 %all_to_all.15 = f16[8,456,128]{2,1,0:T(8,128)(2,1)S(1)} all-to-all(f16[8,456,128]{2,1,0:T(8,128)(2,1)S(1)} %convert_element_type.12), channel_id=1, replica_groups=mesh['z'=8,'x_lo'=2,'core'=2,'x_hi'=2,'y'=4] {'x_hi','y'}, dimensions={0} | all-to-all | bytes 1867776 | tf_op jit(solution)/shard_map/depth_exchange/all_to_all | solution.py:225
  28.6 0.0 copy-start
  28.6 0.1 convert_element_type.13.x_ref
  28.7 0.6 copy-done
  29.3 0.8 expand.1
  30.1 23.9 %all_to_all.16.own_ref = bf16[16,4,16,256]{3,2,1,0:T(8,128)(2,1)S(1)} all-to-all(bf16[16,4,16,256]{3,2,1,0:T(8,128)(2,1)S(1)} %expand.1), channel_id=1, replica_groups=mesh['z'=8,'x_lo'=2,'core'=2,'x_hi'=2,'y'=4] {'z','x_lo'}, dimensions={0} | all-to-all | bytes 1048576 | tf_op jit(solution)/shard_map/row_exchange/all_to_all | solution.py:237
  54.0 0.0 collective-permute-start
  54.1 1.9 %collective-permute-done.other_ref = bf16[16,4,16,256]{3,2,1,0:T(8,128)(2,1)S(1)} collective-permute-done((bf16[16,4,16,256]{3,2,1,0:T(8,128)(2,1)S(1)}, bf16[16,4,16,256]{3,2,1,0:T(8,128)(2,1)S(1)}, u32[]{:S(2)}, u32[]{:S(2)}) %collective-permute-start) | collective-permute-done | bytes 524320 | tf_op jit(solution)/shard_map/core_swap/ppermute | solution.py:239
  56.0 0.8 gram.1
  56.8 23.4 %all_to_all.17 = f16[128,8,128]{2,1,0:T(8,128)(2,1)S(1)} all-to-all(f16[128,8,128]{2,1,0:T(8,128)(2,1)S(1)} %convert_element_type.14), channel_id=1, replica_groups=mesh['z'=8,'x_lo'=2,'core'=2,'x_hi'=2,'y'=4] {'z','x_lo','x_hi','y'}, dimensions={0} | all-to-all | bytes 524288 | tf_op jit(solution)/shard_map/gram_exchange/all_to_all | solution.py:225
  80.3 1.0 %finish.1 = f32[14,56]{1,0:T(8,128)} custom-call(f32[128,8,128]{2,1,0:T(8,128)S(1)} %convert_element_type.15.x_ref), custom_call_target="tpu_custom_call" | custom-call | tf_op jit(solution)/shard_map/finish/pallas_call | solution.py:217
  (2 shorter events, 0.1 us)
Async XLA Ops:
  28.6 0.8 copy-start
  54.0 1.9 %collective-permute-start = (bf16[16,4,16,256]{3,2,1,0:T(8,128)(2,1)S(1)}, bf16[16,4,16,256]{3,2,1,0:T(8,128)(2,1)S(1)}, u32[]{:S(2)}, u32[]{:S(2)}) collective-permute-start(bf16[16,4,16,256]{3,2,1,0:T(8,128)(2,1)S(1)} %all_to_all.16.own_ref), channel_id=1, source_target_pairs={{0,8},{8,0},{1,9},{9,1},{2,10},{10,2},{3,11},{11,3},{4,12},{12,4},... | collective-permute-start | bytes 1572872 | tf_op jit(solution)/shard_map/core_swap/ppermute | solution.py:239

commit v5 on v4

--- a/solution.py
+++ b/solution.py
@@ -15,7 +15,6 @@
 CELLS = I3 * I4 * I5
 INNER = I4 * I5
 PAIR = R4 * R5
-MAIN = 256
 WIDE = R3 * DEPTH // 8
 PAD = 16
 ROWS_STEP = 2
@@ -34,8 +33,20 @@
     return lax.dot_general(left, right, (((1,), (0,)), ((), ())), preferred_element_type=F32)
 
 
-def exponent(peak):
-    return jnp.floor(jnp.log2(jnp.maximum(peak, 1e-30))) - 14.0
+def exponent(peak, target):
+    return jnp.floor(jnp.log2(jnp.maximum(peak, 1e-30))) - target
+
+
+def encode(value):
+    square = value * value
+    fourth = square * square
+    return (fourth * fourth * value).astype(BF16)
+
+
+def decode(code, level):
+    wide = code.astype(F32)
+    size = jnp.exp2(jnp.log2(jnp.abs(wide)) * (1.0 / 9.0) + level)
+    return jnp.where(wide == 0.0, 0.0, jnp.where(wide < 0.0, -size, size))
 
 
 def exact_dot(left, right, dims):
@@ -44,10 +55,15 @@
     )
 
 
-def squeeze_kernel(t_hbm, f3_hbm, f4t_hbm, f5_hbm, out_ref, t_ref, f3_ref, f4t_ref, f5_ref, main_h, main_l, rest, mix_h, mix_l, sems):
+def squeeze_kernel(
+    t_hbm, f3_hbm, f4t_hbm, f5_hbm, out_hbm,
+    t_ref, f3_ref, f4t_ref, f5_ref, rows_ref, main_h, mix_h, mix_l, code_ref, sems, out_sems,
+):
     small = [
         pltpu.make_async_copy(src, dst, sems.at[ROWS + n])
-        for n, (src, dst) in enumerate(((f3_hbm, f3_ref), (f4t_hbm, f4t_ref), (f5_hbm, f5_ref)))
+        for n, (src, dst) in enumerate(
+            ((f3_hbm, f3_ref), (f4t_hbm, f4t_ref), (f5_hbm, f5_ref))
+        )
     ]
     loads = [pltpu.make_async_copy(t_hbm.at[i], t_ref.at[i], sems.at[i]) for i in range(ROWS)]
     for copy in small + loads:
@@ -67,14 +83,6 @@
     high, low = split(pair)
     main_h[:, :PAIR] = high
     main_h[:, PAIR:] = low
-    tail_h, tail_l = high[MAIN:], low[MAIN:]
-    rest[...] = jnp.concatenate(
-        [
-            jnp.concatenate([tail_h, tail_l], axis=1),
-            jnp.concatenate([tail_h, jnp.zeros_like(tail_l)], axis=1),
-        ],
-        axis=0,
-    )
     size = R3 * DEPTH
     a_row = lax.broadcasted_iota(jnp.int32, (size, I3), 0) // DEPTH
     a_col = lax.broadcasted_iota(jnp.int32, (size, I3), 1)
@@ -105,15 +113,20 @@
             inner_h, inner_l = split(stack[n * size_in:(n + 1) * size_in])
             both = dot(mix_h[...], jnp.concatenate([inner_h, inner_l], axis=1))
             outer = both[:, :PAIR] + (both[:, PAIR:] + dot(mix_l[...], inner_h))
-            out_ref[:, i * WIDE:(i + 1) * WIDE] = outer.reshape(NARROW, WIDE, PAIR)
+            rows_ref[:, i * WIDE:(i + 1) * WIDE] = outer.reshape(NARROW, WIDE, PAIR)
             peak = jnp.maximum(peak, jnp.max(jnp.abs(outer).reshape(-1, 8, PAIR), axis=0))
 
-    level = exponent(jnp.broadcast_to(jnp.max(peak, keepdims=True), (8, PAIR)))
+    level = exponent(jnp.broadcast_to(jnp.max(peak, keepdims=True), (8, PAIR)), 12.0)
     factor = jnp.exp2(-level)
+    stores = []
     for n in range(NARROW):
-        block = out_ref[n, :ROWS * WIDE].reshape(-1, 8, PAIR) * factor
-        out_ref[n, :ROWS * WIDE] = block.reshape(ROWS * WIDE, PAIR)
-        out_ref[n, ROWS * WIDE:] = level
+        block = rows_ref[n].reshape(-1, 8, PAIR) * factor
+        code_ref[n, :ROWS * WIDE] = encode(block).reshape(ROWS * WIDE, PAIR)
+        code_ref[n, ROWS * WIDE:] = jnp.concatenate([level, level], axis=0).astype(BF16)
+        stores.append(pltpu.make_async_copy(code_ref.at[n], out_hbm.at[n], out_sems.at[n]))
+        stores[-1].start()
+    for copy in stores:
+        copy.wait()
 
 
 def squeeze(tensor, f3, f4t, f5):
@@ -122,18 +135,20 @@
     return pl.pallas_call(
         squeeze_kernel,
         in_specs=[hbm] * 4,
-        out_shape=jax.ShapeDtypeStruct((NARROW, ROWS * WIDE + 8, PAIR), F32),
+        out_specs=hbm,
+        out_shape=jax.ShapeDtypeStruct((NARROW, ROWS * WIDE + 16, PAIR), BF16),
         scratch_shapes=[
             pltpu.VMEM((ROWS, DEPTH, CELLS), F32),
             pltpu.VMEM((I3, R3), F32),
             pltpu.VMEM((R4, I4), F32),
             pltpu.VMEM((I5, R5), F32),
+            pltpu.VMEM((NARROW, ROWS * WIDE, PAIR), F32),
             pltpu.VMEM((INNER, 2 * PAIR), BF16),
-            pltpu.VMEM((MAIN, PAIR), BF16),
-            pltpu.VMEM((2 * (INNER - MAIN), 2 * PAIR), BF16),
             pltpu.VMEM((size, size), BF16),
             pltpu.VMEM((size, size), BF16),
+            pltpu.VMEM((NARROW, ROWS * WIDE + 16, PAIR), BF16),
             pltpu.SemaphoreType.DMA((ROWS + 3,)),
+            pltpu.SemaphoreType.DMA((NARROW,)),
         ],
         compiler_params=pltpu.CompilerParams(vmem_limit_bytes=61 * 1024 * 1024),
     )(tensor, f3, f4t, f5)
@@ -142,10 +157,10 @@
 def expand_kernel(x_ref, f2t_ref, out_ref, rows_ref):
     high, low = split(f2t_ref[...])
     left = jnp.concatenate([high, low], axis=0)
-    factor = jnp.exp2(x_ref[:, ROWS * WIDE:])
+    level = x_ref[:, ROWS * WIDE:].astype(F32)[:, None]
     for i in range(ROWS):
-        piece = x_ref[:, i * WIDE:(i + 1) * WIDE].reshape(NARROW, WIDE // 8, 8, PAIR) * factor[:, None]
-        piece_h, piece_l = split(piece.reshape(NARROW, WIDE, PAIR))
+        code = x_ref[:, i * WIDE:(i + 1) * WIDE].reshape(NARROW, WIDE // 16, 16, PAIR)
+        piece_h, piece_l = split(decode(code, level).reshape(NARROW, WIDE, PAIR))
         right_h, right_l = (
             jnp.concatenate(
                 [p[:, h * DEPTH:(h + 1) * DEPTH].reshape(NARROW * DEPTH, PAIR) for h in range(2)], axis=1
@@ -153,7 +168,7 @@
             for p in (piece_h, piece_l)
         )
         both = dot(left, right_h)
-        core = both[:R2] + (both[R2:] + dot(high, right_l))
+        core = both[:R2] + (both[R2:] + dot(left[:R2], right_l))
         for h in range(2):
             rows_ref[h, pl.ds(i, R2, stride=PAD), :] = core[:, h * PAIR:(h + 1) * PAIR]
     keep = lax.broadcasted_iota(jnp.int32, (R2, PAD, PAIR), 1) < ROWS
@@ -181,7 +196,7 @@
         part = lax.dot_general(left, right, (((1,), (1,)), ((), ())), preferred_element_type=F32)
         total = part if total is None else total + part
     peak = jnp.max(jnp.abs(total), axis=0, keepdims=True)
-    level = exponent(jnp.broadcast_to(jnp.max(peak, axis=1, keepdims=True), (8, 128)))
+    level = exponent(jnp.broadcast_to(jnp.max(peak, axis=1, keepdims=True), (8, 128)), 14.0)
     total = total * jnp.exp2(-level[:1, :1])
     first = lax.broadcasted_iota(jnp.int32, (8, 128), 1) < 64
     last = lax.broadcasted_iota(jnp.int32, (8, 128), 0) == 7
@@ -221,16 +236,11 @@
     )(parts)
 
 
-def exchange(value, axes):
-    sent = lax.all_to_all(value.astype(F16), axes, 0, 0, tiled=True)
-    return sent.astype(F32)
-
-
 def per_device(tensor, f2, f3, f4, f5):
     with jax.named_scope("squeeze"):
         reduced = squeeze(tensor, f3, f4.T, f5)
     with jax.named_scope("depth_exchange"):
-        gathered = exchange(reduced, ("x_hi", "y"))
+        gathered = lax.all_to_all(reduced, ("x_hi", "y"), 0, 0, tiled=True)
     with jax.named_scope("expand"):
         core = expand(gathered, f2.T)
     with jax.named_scope("row_exchange"):
@@ -240,7 +250,7 @@
     with jax.named_scope("gram"):
         parts = gram(rows, other)
     with jax.named_scope("gram_exchange"):
-        parts = exchange(parts, ("z", "x_lo", "x_hi", "y"))
+        parts = lax.all_to_all(parts.astype(F16), ("z", "x_lo", "x_hi", "y"), 0, 0, tiled=True).astype(F32)
     with jax.named_scope("finish"):
         return finish(parts)
 

time: 81.6 us -> 79.9 us (0.979)
  other arithmetic: 1.83 us -> 0.07 us
    convert_element_type x4 -> x2, other arithmetic: 1.83 us -> 0.07 us  [the longest x1 0.04 us: per_device(): parts.astype(F16)]
where the time goes in v5:
time: 79.9 us; the launch traced here: 79.7 us
  blocking collectives  68 us (85%)
  Pallas kernels  9.66 us (12%)
  waiting for transfers between devices  1.91 us (2%)
    all_to_all x1, blocking collectives, per_device(): rows = lax.all_to_all(core, ('z', 'x_lo'), 0, 0, tiled=True)  23.9 us
    all_to_all x1, blocking collectives, per_device(): lax.all_to_all(parts.astype(F16), ('z', 'x_lo', 'x_hi', 'y'), 0, 0, tiled...  23.4 us
    all_to_all x1, blocking collectives, per_device(): gathered = lax.all_to_all(reduced, ('x_hi', 'y'), 0, 0, tiled=True)  20.7 us
    pallas_call x1, Pallas kernels, squeeze(): pl.pallas_call(squeeze_kernel, in_specs=[hbm] * 4, out_specs=hbm, out_sha...  6.46 us
    ppermute x1, waiting for transfers between devices, per_device(): other = lax.ppermute(rows, 'core', [(0, 1), (1, 0)])  1.91 us
  transfers between devices with their start and end apart: 1, of which 1 were waited for; matrix products, arithmetic and copies ran while one was open for 0% of the time, Pallas kernels for 0%

profile of v5, /device:TPU:6, one launch (start us, length us, event | category | flops | bytes accessed | tf_op | source)
XLA Modules:
  0.0 79.7 jit_solution(2358725674390535743)
XLA Ops:
  0.0 0.0 copy-start
  0.0 6.5 %squeeze.1 = bf16[8,464,128]{2,1,0:T(8,128)(2,1)} custom-call(f32[14,16,4224]{2,1,0:T(8,128)} %t_hbm.1, f32[16,16]{1,0:T(8,128)} %f3_hbm.1, f32[16,33]{1,0:T(8,128)} %bitcast.3, f32[8,8]{1,0:T(8,128)} %f5_hbm.1), custom_call_target="tpu_custom_call" | custom-call | tf_op jit(solution)/shard_map/squeeze/pallas_call | solution.py:135
  6.5 20.7 %all_to_all.15.x_ref = bf16[8,464,128]{2,1,0:T(8,128)(2,1)S(1)} all-to-all(bf16[8,464,128]{2,1,0:T(8,128)(2,1)} %squeeze.1), channel_id=1, replica_groups=mesh['z'=8,'x_lo'=2,'core'=2,'x_hi'=2,'y'=4] {'x_hi','y'}, dimensions={0} | all-to-all | bytes 1900544 | tf_op jit(solution)/shard_map/depth_exchange/all_to_all | solution.py:243
  27.2 0.0 copy-done
  27.2 1.4 %expand.1 = bf16[16,4,16,256]{3,2,1,0:T(8,128)(2,1)S(1)} custom-call(bf16[8,464,128]{2,1,0:T(8,128)(2,1)S(1)} %all_to_all.15.x_ref, f32[64,128]{1,0:T(8,128)S(1)} %bitcast.2), custom_call_target="tpu_custom_call" | custom-call | tf_op jit(solution)/shard_map/expand/pallas_call | solution.py:181
  28.6 23.9 %all_to_all.16.own_ref = bf16[16,4,16,256]{3,2,1,0:T(8,128)(2,1)S(1)} all-to-all(bf16[16,4,16,256]{3,2,1,0:T(8,128)(2,1)S(1)} %expand.1), channel_id=1, replica_groups=mesh['z'=8,'x_lo'=2,'core'=2,'x_hi'=2,'y'=4] {'z','x_lo'}, dimensions={0} | all-to-all | bytes 1048576 | tf_op jit(solution)/shard_map/row_exchange/all_to_all | solution.py:247
  52.5 0.0 collective-permute-start
  52.5 1.9 %collective-permute-done.other_ref = bf16[16,4,16,256]{3,2,1,0:T(8,128)(2,1)S(1)} collective-permute-done((bf16[16,4,16,256]{3,2,1,0:T(8,128)(2,1)S(1)}, bf16[16,4,16,256]{3,2,1,0:T(8,128)(2,1)S(1)}, u32[]{:S(2)}, u32[]{:S(2)}) %collective-permute-start) | collective-permute-done | bytes 524320 | tf_op jit(solution)/shard_map/core_swap/ppermute | solution.py:249
  54.4 0.8 gram.1
  55.2 23.4 %all_to_all.17 = f16[128,8,128]{2,1,0:T(8,128)(2,1)S(1)} all-to-all(f16[128,8,128]{2,1,0:T(8,128)(2,1)S(1)} %convert_element_type.6), channel_id=1, replica_groups=mesh['z'=8,'x_lo'=2,'core'=2,'x_hi'=2,'y'=4] {'z','x_lo','x_hi','y'}, dimensions={0} | all-to-all | bytes 524288 | tf_op jit(solution)/shard_map/gram_exchange/all_to_all | solution.py:253
  78.7 1.0 %finish.1 = f32[14,56]{1,0:T(8,128)} custom-call(f32[128,8,128]{2,1,0:T(8,128)S(1)} %convert_element_type.7.x_ref), custom_call_target="tpu_custom_call" | custom-call | tf_op jit(solution)/shard_map/finish/pallas_call | solution.py:232
  (2 shorter events, 0.1 us)
Async XLA Ops:
  0.0 27.2 %copy-start = (f32[128,64]{0,1:T(8,128)S(1)}, f32[128,64]{0,1:T(8,128)}, u32[]{:S(2)}) copy-start(f32[128,64]{0,1:T(8,128)} %param.6) | copy-start | bytes 98308
  52.5 1.9 %collective-permute-start = (bf16[16,4,16,256]{3,2,1,0:T(8,128)(2,1)S(1)}, bf16[16,4,16,256]{3,2,1,0:T(8,128)(2,1)S(1)}, u32[]{:S(2)}, u32[]{:S(2)}) collective-permute-start(bf16[16,4,16,256]{3,2,1,0:T(8,128)(2,1)S(1)} %all_to_all.16.own_ref), channel_id=1, source_target_pairs={{0,8},{8,0},{1,9},{9,1},{2,10},{10,2},{3,11},{11,3},{4,12},{12,4},... | collective-permute-start | bytes 1572872 | tf_op jit(solution)/shard_map/core_swap/ppermute | solution.py:249

commit v6 on v5

--- a/solution.py
+++ b/solution.py
@@ -21,6 +21,8 @@
 Z, XL, CORE, XH, Y = 8, 2, 2, 2, 4
 NARROW = XH * Y
 GROUPS = Z * XL
+SLICES = R2 // GROUPS * 2
+BLOCK = SLICES * ROWS
 VMEM_LIMIT = 32 * 1024 * 1024
 
 
@@ -56,8 +58,8 @@
 
 
 def squeeze_kernel(
-    t_hbm, f3_hbm, f4t_hbm, f5_hbm, out_hbm,
-    t_ref, f3_ref, f4t_ref, f5_ref, rows_ref, main_h, mix_h, mix_l, code_ref, sems, out_sems,
+    t_hbm, f3_hbm, f4t_hbm, f5_hbm, out_ref,
+    t_ref, f3_ref, f4t_ref, f5_ref, rows_ref, main_h, mix_h, mix_l, sems,
 ):
     small = [
         pltpu.make_async_copy(src, dst, sems.at[ROWS + n])
@@ -118,15 +120,10 @@
 
     level = exponent(jnp.broadcast_to(jnp.max(peak, keepdims=True), (8, PAIR)), 12.0)
     factor = jnp.exp2(-level)
-    stores = []
     for n in range(NARROW):
         block = rows_ref[n].reshape(-1, 8, PAIR) * factor
-        code_ref[n, :ROWS * WIDE] = encode(block).reshape(ROWS * WIDE, PAIR)
-        code_ref[n, ROWS * WIDE:] = jnp.concatenate([level, level], axis=0).astype(BF16)
-        stores.append(pltpu.make_async_copy(code_ref.at[n], out_hbm.at[n], out_sems.at[n]))
-        stores[-1].start()
-    for copy in stores:
-        copy.wait()
+        out_ref[n, :ROWS * WIDE] = encode(block).reshape(ROWS * WIDE, PAIR)
+        out_ref[n, ROWS * WIDE:] = jnp.concatenate([level, level], axis=0).astype(BF16)
 
 
 def squeeze(tensor, f3, f4t, f5):
@@ -135,8 +132,8 @@
     return pl.pallas_call(
         squeeze_kernel,
         in_specs=[hbm] * 4,
-        out_specs=hbm,
-        out_shape=jax.ShapeDtypeStruct((NARROW, ROWS * WIDE + 16, PAIR), BF16),
+        out_shape=pltpu.VMEM((NARROW, ROWS * WIDE + 16, PAIR), BF16),
+        out_specs=pl.BlockSpec(memory_space=pltpu.VMEM),
         scratch_shapes=[
             pltpu.VMEM((ROWS, DEPTH, CELLS), F32),
             pltpu.VMEM((I3, R3), F32),
@@ -146,11 +143,9 @@
             pltpu.VMEM((INNER, 2 * PAIR), BF16),
             pltpu.VMEM((size, size), BF16),
             pltpu.VMEM((size, size), BF16),
-            pltpu.VMEM((NARROW, ROWS * WIDE + 16, PAIR), BF16),
             pltpu.SemaphoreType.DMA((ROWS + 3,)),
-            pltpu.SemaphoreType.DMA((NARROW,)),
         ],
-        compiler_params=pltpu.CompilerParams(vmem_limit_bytes=61 * 1024 * 1024),
+        compiler_params=pltpu.CompilerParams(vmem_limit_bytes=58 * 1024 * 1024),
     )(tensor, f3, f4t, f5)
 
 
@@ -170,29 +165,39 @@
         both = dot(left, right_h)
         core = both[:R2] + (both[R2:] + dot(left[:R2], right_l))
         for h in range(2):
-            rows_ref[h, pl.ds(i, R2, stride=PAD), :] = core[:, h * PAIR:(h + 1) * PAIR]
-    keep = lax.broadcasted_iota(jnp.int32, (R2, PAD, PAIR), 1) < ROWS
-    for h in range(2):
-        block = jnp.where(keep, rows_ref[h].reshape(R2, PAD, PAIR), 0.0)
-        out_ref[:, :, :, h * PAIR:(h + 1) * PAIR] = block.astype(BF16).reshape(GROUPS, -1, PAD, PAIR)
+            rows_ref[pl.ds(h * ROWS + i, R2, stride=2 * ROWS), :] = core[:, h * PAIR:(h + 1) * PAIR]
+    out_ref[...] = rows_ref[...].astype(BF16).reshape(GROUPS, BLOCK, PAIR)
 
 
 def expand(gathered, f2t):
     return pl.pallas_call(
         expand_kernel,
-        out_shape=jax.ShapeDtypeStruct((GROUPS, R2 // GROUPS, PAD, 2 * PAIR), BF16),
-        scratch_shapes=[pltpu.VMEM((2, R2 * PAD, PAIR), F32)],
+        out_shape=jax.ShapeDtypeStruct((GROUPS, BLOCK, PAIR), BF16),
+        scratch_shapes=[pltpu.VMEM((R2 * 2 * ROWS, PAIR), F32)],
         compiler_params=pltpu.CompilerParams(vmem_limit_bytes=VMEM_LIMIT),
     )(gathered, f2t)
 
 
 def gram_kernel(own_ref, other_ref, out_ref):
+    row = lax.broadcasted_iota(jnp.int32, (SLICES * PAD, BLOCK), 0)
+    col = lax.broadcasted_iota(jnp.int32, (SLICES * PAD, BLOCK), 1)
+    spread = ((row % PAD < ROWS) & (row // PAD * ROWS + row % PAD == col)).astype(BF16)
+    padded = [
+        dot(spread, jnp.concatenate([own_ref[g], other_ref[g]], axis=1)).astype(BF16) for g in range(GROUPS)
+    ]
     total = None
-    for q in range(R2 // GROUPS):
-        left = own_ref[:, q].reshape(GROUPS * PAD, 2 * PAIR)
-        right = jnp.concatenate(
-            [ref[g, q] for g in range(GROUPS) for ref in (own_ref, other_ref)], axis=0
+    for q in range(0, SLICES, 2):
+        own, other = (
+            [
+                jnp.concatenate(
+                    [both[p * PAD:(p + 1) * PAD, c * PAIR:(c + 1) * PAIR] for p in (q, q + 1)], axis=1
+                )
+                for both in padded
+            ]
+            for c in range(CORE)
         )
+        left = jnp.concatenate(own, axis=0)
+        right = jnp.concatenate([part for pair in zip(own, other) for part in pair], axis=0)
         part = lax.dot_general(left, right, (((1,), (1,)), ((), ())), preferred_element_type=F32)
         total = part if total is None else total + part
     peak = jnp.max(jnp.abs(total), axis=0, keepdims=True)

time: 79.9 us -> 77.5 us (0.970)
  blocking collectives: 68 us -> 66.4 us
    all_to_all x1, blocking collectives: 23.9 us -> 22.6 us  [per_device(): rows = lax.all_to_all(core, ('z', 'x_lo'), 0, 0, tiled=True)]
    pallas_call x2, Pallas kernels: 7.85 us -> 6.82 us  [the longest x1 5.62 us: squeeze(): pl.pallas_call(squeeze_kernel, in_specs=[hbm] * 4, out_shape=pltpu.VMEM((...]
where the time goes in v6:
time: 77.5 us; the launch traced here: 77.3 us
  blocking collectives  66.4 us (86%)
  Pallas kernels  8.97 us (12%)
  waiting for transfers between devices  1.81 us (2%)
    all_to_all x1, blocking collectives, per_device(): lax.all_to_all(parts.astype(F16), ('z', 'x_lo', 'x_hi', 'y'), 0, 0, tiled...  23.3 us
    all_to_all x1, blocking collectives, per_device(): rows = lax.all_to_all(core, ('z', 'x_lo'), 0, 0, tiled=True)  22.6 us
    all_to_all x1, blocking collectives, per_device(): gathered = lax.all_to_all(reduced, ('x_hi', 'y'), 0, 0, tiled=True)  20.5 us
    pallas_call x1, Pallas kernels, squeeze(): pl.pallas_call(squeeze_kernel, in_specs=[hbm] * 4, out_shape=pltpu.VMEM((...  5.62 us
    ppermute x1, waiting for transfers between devices, per_device(): other = lax.ppermute(rows, 'core', [(0, 1), (1, 0)])  1.81 us
  transfers between devices with their start and end apart: 1, of which 1 were waited for; matrix products, arithmetic and copies ran while one was open for 0% of the time, Pallas kernels for 0%

profile of v6, /device:TPU:6, one launch (start us, length us, event | category | flops | bytes accessed | tf_op | source)
XLA Modules:
  0.0 77.3 jit_solution(7658448067863998565)
XLA Ops:
  0.0 0.0 copy-start
  0.0 5.6 %squeeze.1 = bf16[8,464,128]{2,1,0:T(8,128)(2,1)S(1)} custom-call(f32[14,16,4224]{2,1,0:T(8,128)} %t_hbm.1, f32[16,16]{1,0:T(8,128)} %f3_hbm.1, f32[16,33]{1,0:T(8,128)} %bitcast.3, f32[8,8]{1,0:T(8,128)} %f5_hbm.1), custom_call_target="tpu_custom_call" | custom-call | tf_op jit(solution)/shard_map/squeeze/pallas_call | solution.py:132
  5.6 20.5 %all_to_all.15.x_ref = bf16[8,464,128]{2,1,0:T(8,128)(2,1)S(1)} all-to-all(bf16[8,464,128]{2,1,0:T(8,128)(2,1)S(1)} %squeeze.1), channel_id=1, replica_groups=mesh['z'=8,'x_lo'=2,'core'=2,'x_hi'=2,'y'=4] {'x_hi','y'}, dimensions={0} | all-to-all | bytes 1900544 | tf_op jit(solution)/shard_map/depth_exchange/all_to_all | solution.py:248
  26.1 0.0 copy-done
  26.1 1.2 %expand.1 = bf16[16,112,128]{2,1,0:T(8,128)(2,1)S(1)} custom-call(bf16[8,464,128]{2,1,0:T(8,128)(2,1)S(1)} %all_to_all.15.x_ref, f32[64,128]{1,0:T(8,128)S(1)} %bitcast.2), custom_call_target="tpu_custom_call" | custom-call | tf_op jit(solution)/shard_map/expand/pallas_call | solution.py:173
  27.3 22.6 %all_to_all.16.own_ref = bf16[16,112,128]{2,1,0:T(8,128)(2,1)S(1)} all-to-all(bf16[16,112,128]{2,1,0:T(8,128)(2,1)S(1)} %expand.1), channel_id=1, replica_groups=mesh['z'=8,'x_lo'=2,'core'=2,'x_hi'=2,'y'=4] {'z','x_lo'}, dimensions={0} | all-to-all | bytes 917504 | tf_op jit(solution)/shard_map/row_exchange/all_to_all | solution.py:252
  50.0 0.0 collective-permute-start
  50.0 1.8 %collective-permute-done.other_ref = bf16[16,112,128]{2,1,0:T(8,128)(2,1)S(1)} collective-permute-done((bf16[16,112,128]{2,1,0:T(8,128)(2,1)S(1)}, bf16[16,112,128]{2,1,0:T(8,128)(2,1)S(1)}, u32[]{:S(2)}, u32[]{:S(2)}) %collective-permute-start) | collective-permute-done | bytes 458784 | tf_op jit(solution)/shard_map/core_swap/ppermute | solution.py:254
  51.8 1.1 %gram.1 = f32[128,8,128]{2,1,0:T(8,128)S(1)} custom-call(bf16[16,112,128]{2,1,0:T(8,128)(2,1)S(1)} %all_to_all.16.own_ref, bf16[16,112,128]{2,1,0:T(8,128)(2,1)S(1)} %collective-permute-done.other_ref), custom_call_target="tpu_custom_call" | custom-call | tf_op jit(solution)/shard_map/gram/pallas_call | solution.py:217
  53.0 23.3 %all_to_all.17 = f16[128,8,128]{2,1,0:T(8,128)(2,1)S(1)} all-to-all(f16[128,8,128]{2,1,0:T(8,128)(2,1)S(1)} %convert_element_type.6), channel_id=1, replica_groups=mesh['z'=8,'x_lo'=2,'core'=2,'x_hi'=2,'y'=4] {'z','x_lo','x_hi','y'}, dimensions={0} | all-to-all | bytes 524288 | tf_op jit(solution)/shard_map/gram_exchange/all_to_all | solution.py:258
  76.3 1.0 %finish.1 = f32[14,56]{1,0:T(8,128)} custom-call(f32[128,8,128]{2,1,0:T(8,128)S(1)} %convert_element_type.7.x_ref), custom_call_target="tpu_custom_call" | custom-call | tf_op jit(solution)/shard_map/finish/pallas_call | solution.py:237
  (2 shorter events, 0.1 us)
Async XLA Ops:
  0.0 26.1 %copy-start = (f32[128,64]{0,1:T(8,128)S(1)}, f32[128,64]{0,1:T(8,128)}, u32[]{:S(2)}) copy-start(f32[128,64]{0,1:T(8,128)} %param.6) | copy-start | bytes 98308
  50.0 1.8 %collective-permute-start = (bf16[16,112,128]{2,1,0:T(8,128)(2,1)S(1)}, bf16[16,112,128]{2,1,0:T(8,128)(2,1)S(1)}, u32[]{:S(2)}, u32[]{:S(2)}) collective-permute-start(bf16[16,112,128]{2,1,0:T(8,128)(2,1)S(1)} %all_to_all.16.own_ref), channel_id=1, source_target_pairs={{0,8},{8,0},{1,9},{9,1},{2,10},{10,2},{3,11},{11,3},{4,12},{12,4},... | collective-permute-start | bytes 1376264 | tf_op jit(solution)/shard_map/core_swap/ppermute | solution.py:254

commit v7 on v6

--- a/solution.py
+++ b/solution.py
@@ -15,13 +15,15 @@
 CELLS = I3 * I4 * I5
 INNER = I4 * I5
 PAIR = R4 * R5
-WIDE = R3 * DEPTH // 8
+WIDE = DEPTH
 PAD = 16
+SHIFT = 2.0 ** 24
 ROWS_STEP = 2
 Z, XL, CORE, XH, Y = 8, 2, 2, 2, 4
 NARROW = XH * Y
+FIRST = NARROW * XL
 GROUPS = Z * XL
-SLICES = R2 // GROUPS * 2
+SLICES = R2 // Z * XL
 BLOCK = SLICES * ROWS
 VMEM_LIMIT = 32 * 1024 * 1024
 
@@ -35,19 +37,18 @@
     return lax.dot_general(left, right, (((1,), (0,)), ((), ())), preferred_element_type=F32)
 
 
-def exponent(peak, target):
-    return jnp.floor(jnp.log2(jnp.maximum(peak, 1e-30))) - target
+def exponent(peak):
+    return jnp.floor(jnp.log2(jnp.maximum(peak, 1e-30))) - 14.0
 
 
 def encode(value):
-    square = value * value
-    fourth = square * square
-    return (fourth * fourth * value).astype(BF16)
-
-
-def decode(code, level):
+    wide = value * SHIFT
+    return (wide * wide * wide).astype(BF16)
+
+
+def decode(code):
     wide = code.astype(F32)
-    size = jnp.exp2(jnp.log2(jnp.abs(wide)) * (1.0 / 9.0) + level)
+    size = jnp.exp2(jnp.log2(jnp.abs(wide)) * (1.0 / 3.0)) * (1.0 / SHIFT)
     return jnp.where(wide == 0.0, 0.0, jnp.where(wide < 0.0, -size, size))
 
 
@@ -59,7 +60,7 @@
 
 def squeeze_kernel(
     t_hbm, f3_hbm, f4t_hbm, f5_hbm, out_ref,
-    t_ref, f3_ref, f4t_ref, f5_ref, rows_ref, main_h, mix_h, mix_l, sems,
+    t_ref, f3_ref, f4t_ref, f5_ref, main_h, mix_h, mix_l, sems,
 ):
     small = [
         pltpu.make_async_copy(src, dst, sems.at[ROWS + n])
@@ -100,7 +101,6 @@
     mix_l[...] = low
 
     size_in = R3 * DEPTH
-    peak = jnp.zeros((8, PAIR), F32)
     for base in range(0, ROWS, 7):
         group = range(base, base + 7)
         for i in group:
@@ -115,15 +115,7 @@
             inner_h, inner_l = split(stack[n * size_in:(n + 1) * size_in])
             both = dot(mix_h[...], jnp.concatenate([inner_h, inner_l], axis=1))
             outer = both[:, :PAIR] + (both[:, PAIR:] + dot(mix_l[...], inner_h))
-            rows_ref[:, i * WIDE:(i + 1) * WIDE] = outer.reshape(NARROW, WIDE, PAIR)
-            peak = jnp.maximum(peak, jnp.max(jnp.abs(outer).reshape(-1, 8, PAIR), axis=0))
-
-    level = exponent(jnp.broadcast_to(jnp.max(peak, keepdims=True), (8, PAIR)), 12.0)
-    factor = jnp.exp2(-level)
-    for n in range(NARROW):
-        block = rows_ref[n].reshape(-1, 8, PAIR) * factor
-        out_ref[n, :ROWS * WIDE] = encode(block).reshape(ROWS * WIDE, PAIR)
-        out_ref[n, ROWS * WIDE:] = jnp.concatenate([level, level], axis=0).astype(BF16)
+            out_ref[:, i * WIDE:(i + 1) * WIDE] = encode(outer).reshape(FIRST, WIDE, PAIR)
 
 
 def squeeze(tensor, f3, f4t, f5):
@@ -132,14 +124,13 @@
     return pl.pallas_call(
         squeeze_kernel,
         in_specs=[hbm] * 4,
-        out_shape=pltpu.VMEM((NARROW, ROWS * WIDE + 16, PAIR), BF16),
+        out_shape=pltpu.VMEM((FIRST, ROWS * WIDE, PAIR), BF16),
         out_specs=pl.BlockSpec(memory_space=pltpu.VMEM),
         scratch_shapes=[
             pltpu.VMEM((ROWS, DEPTH, CELLS), F32),
             pltpu.VMEM((I3, R3), F32),
             pltpu.VMEM((R4, I4), F32),
             pltpu.VMEM((I5, R5), F32),
-            pltpu.VMEM((NARROW, ROWS * WIDE, PAIR), F32),
             pltpu.VMEM((INNER, 2 * PAIR), BF16),
             pltpu.VMEM((size, size), BF16),
             pltpu.VMEM((size, size), BF16),
@@ -152,27 +143,24 @@
 def expand_kernel(x_ref, f2t_ref, out_ref, rows_ref):
     high, low = split(f2t_ref[...])
     left = jnp.concatenate([high, low], axis=0)
-    level = x_ref[:, ROWS * WIDE:].astype(F32)[:, None]
     for i in range(ROWS):
-        code = x_ref[:, i * WIDE:(i + 1) * WIDE].reshape(NARROW, WIDE // 16, 16, PAIR)
-        piece_h, piece_l = split(decode(code, level).reshape(NARROW, WIDE, PAIR))
+        code = x_ref[:, i * WIDE:(i + 1) * WIDE]
+        pieces = split(decode(code).reshape(NARROW, XL, DEPTH, PAIR))
         right_h, right_l = (
-            jnp.concatenate(
-                [p[:, h * DEPTH:(h + 1) * DEPTH].reshape(NARROW * DEPTH, PAIR) for h in range(2)], axis=1
-            )
-            for p in (piece_h, piece_l)
+            jnp.concatenate([p[:, x].reshape(NARROW * DEPTH, PAIR) for x in range(XL)], axis=1)
+            for p in pieces
         )
         both = dot(left, right_h)
         core = both[:R2] + (both[R2:] + dot(left[:R2], right_l))
         for h in range(2):
             rows_ref[pl.ds(h * ROWS + i, R2, stride=2 * ROWS), :] = core[:, h * PAIR:(h + 1) * PAIR]
-    out_ref[...] = rows_ref[...].astype(BF16).reshape(GROUPS, BLOCK, PAIR)
+    out_ref[...] = rows_ref[...].astype(BF16).reshape(Z, BLOCK, PAIR)
 
 
 def expand(gathered, f2t):
     return pl.pallas_call(
         expand_kernel,
-        out_shape=jax.ShapeDtypeStruct((GROUPS, BLOCK, PAIR), BF16),
+        out_shape=jax.ShapeDtypeStruct((Z, BLOCK, PAIR), BF16),
         scratch_shapes=[pltpu.VMEM((R2 * 2 * ROWS, PAIR), F32)],
         compiler_params=pltpu.CompilerParams(vmem_limit_bytes=VMEM_LIMIT),
     )(gathered, f2t)
@@ -183,16 +171,17 @@
     col = lax.broadcasted_iota(jnp.int32, (SLICES * PAD, BLOCK), 1)
     spread = ((row % PAD < ROWS) & (row // PAD * ROWS + row % PAD == col)).astype(BF16)
     padded = [
-        dot(spread, jnp.concatenate([own_ref[g], other_ref[g]], axis=1)).astype(BF16) for g in range(GROUPS)
+        dot(spread, jnp.concatenate([own_ref[g], other_ref[g]], axis=1)).astype(BF16) for g in range(Z)
     ]
     total = None
-    for q in range(0, SLICES, 2):
+    for q in range(0, SLICES, 2 * XL):
         own, other = (
             [
                 jnp.concatenate(
-                    [both[p * PAD:(p + 1) * PAD, c * PAIR:(c + 1) * PAIR] for p in (q, q + 1)], axis=1
+                    [both[p * PAD:(p + 1) * PAD, c * PAIR:(c + 1) * PAIR] for p in (q + x, q + x + XL)], axis=1
                 )
                 for both in padded
+                for x in range(XL)
             ]
             for c in range(CORE)
         )
@@ -201,7 +190,7 @@
         part = lax.dot_general(left, right, (((1,), (1,)), ((), ())), preferred_element_type=F32)
         total = part if total is None else total + part
     peak = jnp.max(jnp.abs(total), axis=0, keepdims=True)
-    level = exponent(jnp.broadcast_to(jnp.max(peak, axis=1, keepdims=True), (8, 128)), 14.0)
+    level = exponent(jnp.broadcast_to(jnp.max(peak, axis=1, keepdims=True), (8, 128)))
     total = total * jnp.exp2(-level[:1, :1])
     first = lax.broadcasted_iota(jnp.int32, (8, 128), 1) < 64
     last = lax.broadcasted_iota(jnp.int32, (8, 128), 0) == 7
@@ -245,11 +234,11 @@
     with jax.named_scope("squeeze"):
         reduced = squeeze(tensor, f3, f4.T, f5)
     with jax.named_scope("depth_exchange"):
-        gathered = lax.all_to_all(reduced, ("x_hi", "y"), 0, 0, tiled=True)
+        gathered = lax.all_to_all(reduced, ("x_hi", "y", "x_lo"), 0, 0, tiled=True)
     with jax.named_scope("expand"):
         core = expand(gathered, f2.T)
     with jax.named_scope("row_exchange"):
-        rows = lax.all_to_all(core, ("z", "x_lo"), 0, 0, tiled=True)
+        rows = lax.all_to_all(core, "z", 0, 0, tiled=True)
     with jax.named_scope("core_swap"):
         other = lax.ppermute(rows, "core", [(0, 1), (1, 0)])
     with jax.named_scope("gram"):

time: 77.5 us -> 76.2 us (0.983)
  blocking collectives: 66.4 us -> 65.6 us
    all_to_all x1, blocking collectives: 23.3 us -> 21.5 us  [per_device(): lax.all_to_all(parts.astype(F16), ('z', 'x_lo', 'x_hi', 'y'), 0, 0, tiled...]
    all_to_all x2, blocking collectives: 43.1 us -> 44.1 us  [the longest x1 23.1 us: per_device(): rows = lax.all_to_all(core, 'z', 0, 0, tiled=True)]
where the time goes in v7:
time: 76.2 us; the launch traced here: 76 us
  blocking collectives  65.6 us (86%)
  Pallas kernels  8.44 us (11%)
  waiting for transfers between devices  1.81 us (2%)
    all_to_all x1, blocking collectives, per_device(): rows = lax.all_to_all(core, 'z', 0, 0, tiled=True)  23.1 us
    all_to_all x1, blocking collectives, per_device(): lax.all_to_all(parts.astype(F16), ('z', 'x_lo', 'x_hi', 'y'), 0, 0, tiled...  21.5 us
    all_to_all x1, blocking collectives, per_device(): gathered = lax.all_to_all(reduced, ('x_hi', 'y', 'x_lo'), 0, 0, tiled=True)  21.1 us
    pallas_call x1, Pallas kernels, squeeze(): pl.pallas_call(squeeze_kernel, in_specs=[hbm] * 4, out_shape=pltpu.VMEM((...  5.06 us
    ppermute x1, waiting for transfers between devices, per_device(): other = lax.ppermute(rows, 'core', [(0, 1), (1, 0)])  1.81 us
  transfers between devices with their start and end apart: 1, of which 1 were waited for; matrix products, arithmetic and copies ran while one was open for 0% of the time, Pallas kernels for 0%

profile of v7, /device:TPU:6, one launch (start us, length us, event | category | flops | bytes accessed | tf_op | source)
XLA Modules:
  0.0 76.0 jit_solution(1312219219591660861)
XLA Ops:
  0.0 0.0 copy-start
  0.0 5.1 %squeeze.1 = bf16[16,224,128]{2,1,0:T(8,128)(2,1)S(1)} custom-call(f32[14,16,4224]{2,1,0:T(8,128)} %t_hbm.1, f32[16,16]{1,0:T(8,128)} %f3_hbm.1, f32[16,33]{1,0:T(8,128)} %bitcast.3, f32[8,8]{1,0:T(8,128)} %f5_hbm.1), custom_call_target="tpu_custom_call" | custom-call | tf_op jit(solution)/shard_map/squeeze/pallas_call | solution.py:124
  5.1 21.1 %all_to_all.15.x_ref = bf16[16,224,128]{2,1,0:T(8,128)(2,1)S(1)} all-to-all(bf16[16,224,128]{2,1,0:T(8,128)(2,1)S(1)} %squeeze.1), channel_id=1, replica_groups=mesh['z'=8,'x_lo'=2,'core'=2,'x_hi'=2,'y'=4] {'x_hi','y','x_lo'}, dimensions={0} | all-to-all | bytes 1835008 | tf_op jit(solution)/shard_map/depth_exchange/all_to_all | solution.py:237
  26.1 0.0 copy-done
  26.1 1.2 %expand.1 = bf16[8,224,128]{2,1,0:T(8,128)(2,1)S(1)} custom-call(bf16[16,224,128]{2,1,0:T(8,128)(2,1)S(1)} %all_to_all.15.x_ref, f32[64,128]{1,0:T(8,128)S(1)} %bitcast.2), custom_call_target="tpu_custom_call" | custom-call | tf_op jit(solution)/shard_map/expand/pallas_call | solution.py:161
  27.4 23.1 %all_to_all.16.own_ref = bf16[8,224,128]{2,1,0:T(8,128)(2,1)S(1)} all-to-all(bf16[8,224,128]{2,1,0:T(8,128)(2,1)S(1)} %expand.1), channel_id=1, replica_groups=mesh['z'=8,'x_lo'=2,'core'=2,'x_hi'=2,'y'=4] {'z'}, dimensions={0} | all-to-all | bytes 917504 | tf_op jit(solution)/shard_map/row_exchange/all_to_all | solution.py:241
  50.4 0.0 collective-permute-start
  50.5 1.8 %collective-permute-done.other_ref = bf16[8,224,128]{2,1,0:T(8,128)(2,1)S(1)} collective-permute-done((bf16[8,224,128]{2,1,0:T(8,128)(2,1)S(1)}, bf16[8,224,128]{2,1,0:T(8,128)(2,1)S(1)}, u32[]{:S(2)}, u32[]{:S(2)}) %collective-permute-start) | collective-permute-done | bytes 458784 | tf_op jit(solution)/shard_map/core_swap/ppermute | solution.py:243
  52.3 1.1 %gram.1 = f32[128,8,128]{2,1,0:T(8,128)S(1)} custom-call(bf16[8,224,128]{2,1,0:T(8,128)(2,1)S(1)} %all_to_all.16.own_ref, bf16[8,224,128]{2,1,0:T(8,128)(2,1)S(1)} %collective-permute-done.other_ref), custom_call_target="tpu_custom_call" | custom-call | tf_op jit(solution)/shard_map/gram/pallas_call | solution.py:206
  53.5 21.5 %all_to_all.17 = f16[128,8,128]{2,1,0:T(8,128)(2,1)S(1)} all-to-all(f16[128,8,128]{2,1,0:T(8,128)(2,1)S(1)} %convert_element_type.6), channel_id=1, replica_groups=mesh['z'=8,'x_lo'=2,'core'=2,'x_hi'=2,'y'=4] {'z','x_lo','x_hi','y'}, dimensions={0} | all-to-all | bytes 524288 | tf_op jit(solution)/shard_map/gram_exchange/all_to_all | solution.py:247
  75.0 1.0 %finish.1 = f32[14,56]{1,0:T(8,128)} custom-call(f32[128,8,128]{2,1,0:T(8,128)S(1)} %convert_element_type.7.x_ref), custom_call_target="tpu_custom_call" | custom-call | tf_op jit(solution)/shard_map/finish/pallas_call | solution.py:226
  (2 shorter events, 0.1 us)
Async XLA Ops:
  0.0 26.1 %copy-start = (f32[128,64]{0,1:T(8,128)S(1)}, f32[128,64]{0,1:T(8,128)}, u32[]{:S(2)}) copy-start(f32[128,64]{0,1:T(8,128)} %param.6) | copy-start | bytes 98308
  50.4 1.8 %collective-permute-start = (bf16[8,224,128]{2,1,0:T(8,128)(2,1)S(1)}, bf16[8,224,128]{2,1,0:T(8,128)(2,1)S(1)}, u32[]{:S(2)}, u32[]{:S(2)}) collective-permute-start(bf16[8,224,128]{2,1,0:T(8,128)(2,1)S(1)} %all_to_all.16.own_ref), channel_id=1, source_target_pairs={{0,8},{8,0},{1,9},{9,1},{2,10},{10,2},{3,11},{11,3},{4,12},{12,4},... | collective-permute-start | bytes 1376264 | tf_op jit(solution)/shard_map/core_swap/ppermute | solution.py:243

commit v8 on v7

--- a/solution.py
+++ b/solution.py
@@ -166,56 +166,99 @@
     )(gathered, f2t)
 
 
-def gram_kernel(own_ref, other_ref, out_ref):
+STEPS = R2 // Z // 2
+
+
+def spread_rows(ref):
     row = lax.broadcasted_iota(jnp.int32, (SLICES * PAD, BLOCK), 0)
     col = lax.broadcasted_iota(jnp.int32, (SLICES * PAD, BLOCK), 1)
     spread = ((row % PAD < ROWS) & (row // PAD * ROWS + row % PAD == col)).astype(BF16)
-    padded = [
-        dot(spread, jnp.concatenate([own_ref[g], other_ref[g]], axis=1)).astype(BF16) for g in range(Z)
+    wide = [
+        dot(spread, jnp.concatenate([ref[g], ref[g + 1]], axis=1)).astype(BF16) for g in range(0, Z, 2)
     ]
-    total = None
-    for q in range(0, SLICES, 2 * XL):
-        own, other = (
+    padded = [both[:, h * PAIR:(h + 1) * PAIR] for both in wide for h in range(2)]
+    span = XL * PAD
+    return [
+        jnp.concatenate(
             [
-                jnp.concatenate(
-                    [both[p * PAD:(p + 1) * PAD, c * PAIR:(c + 1) * PAIR] for p in (q + x, q + x + XL)], axis=1
-                )
-                for both in padded
-                for x in range(XL)
+                jnp.concatenate([p[(2 * q + h) * span:(2 * q + h + 1) * span] for h in range(2)], axis=1)
+                for p in padded
+            ],
+            axis=0,
+        )
+        for q in range(STEPS)
+    ]
+
+
+def outer_product(left, right):
+    return lax.dot_general(left, right, (((1,), (1,)), ((), ())), preferred_element_type=F32)
+
+
+def own_kernel(own_ref, left_ref, total_ref):
+    rows = spread_rows(own_ref)
+    for q in range(STEPS):
+        left_ref[q] = rows[q]
+    total_ref[...] = sum(outer_product(part, part) for part in rows)
+
+
+def own_gram(own):
+    size = GROUPS * PAD
+    return pl.pallas_call(
+        own_kernel,
+        out_shape=(
+            jax.ShapeDtypeStruct((STEPS, size, 2 * PAIR), BF16),
+            jax.ShapeDtypeStruct((size, size), F32),
+        ),
+        cost_estimate=pl.CostEstimate(flops=400_000_000, bytes_accessed=1_200_000, transcendentals=0),
+        compiler_params=pltpu.CompilerParams(vmem_limit_bytes=VMEM_LIMIT),
+    )(own)
+
+
+def gram_kernel(left_ref, own_ref, other_ref, out_ref):
+    rows = spread_rows(other_ref)
+    other = sum(outer_product(left_ref[q], rows[q]) for q in range(STEPS))
+    own = own_ref[...]
+    peak = jnp.max(jnp.maximum(jnp.abs(own), jnp.abs(other)), axis=0, keepdims=True)
+    level = exponent(jnp.broadcast_to(jnp.max(peak, axis=1, keepdims=True), (8, 128)))
+    factor = jnp.exp2(-level)
+    lane = lax.broadcasted_iota(jnp.int32, (8, 128), 1)
+    slot, mark = lane // 32, lane == PAD - 1
+    for g in range(GROUPS):
+        for tile in range(2):
+            cols = slice(tile * 128, tile * 128 + 128)
+            top, bottom = slice(g * PAD, g * PAD + 8), slice(g * PAD + 8, (g + 1) * PAD)
+            parts = [
+                own[top, cols] * factor,
+                pltpu.roll(other[top, cols] * factor, 32, 1),
+                pltpu.roll(own[bottom, cols] * factor, 64, 1),
+                pltpu.roll(other[bottom, cols] * factor, 96, 1),
             ]
-            for c in range(CORE)
-        )
-        left = jnp.concatenate(own, axis=0)
-        right = jnp.concatenate([part for pair in zip(own, other) for part in pair], axis=0)
-        part = lax.dot_general(left, right, (((1,), (1,)), ((), ())), preferred_element_type=F32)
-        total = part if total is None else total + part
-    peak = jnp.max(jnp.abs(total), axis=0, keepdims=True)
-    level = exponent(jnp.broadcast_to(jnp.max(peak, axis=1, keepdims=True), (8, 128)))
-    total = total * jnp.exp2(-level[:1, :1])
-    first = lax.broadcasted_iota(jnp.int32, (8, 128), 1) < 64
-    last = lax.broadcasted_iota(jnp.int32, (8, 128), 0) == 7
-    for g in range(GROUPS):
-        for n in range(0, NARROW, 2):
-            top = total[g * PAD:g * PAD + 8, n * 64:n * 64 + 128]
-            bottom = jnp.where(last, level, total[g * PAD + 8:(g + 1) * PAD, n * 64:n * 64 + 128])
-            out_ref[g * NARROW + n] = jnp.where(first, top, pltpu.roll(bottom, 64, 1))
-            out_ref[g * NARROW + n + 1] = jnp.where(first, pltpu.roll(top, 64, 1), bottom)
-
-
-def gram(own, other):
+            for n in range(4):
+                block = parts[0]
+                for k in range(1, 4):
+                    block = jnp.where(slot == (n + k) % 4, parts[k], block)
+                out_ref[g * NARROW + tile * 4 + n] = jnp.where(mark, level, block)
+
+
+def gram(left, own, other):
     return pl.pallas_call(
         gram_kernel,
         out_shape=jax.ShapeDtypeStruct((GROUPS * NARROW, 8, 128), F32),
         compiler_params=pltpu.CompilerParams(vmem_limit_bytes=VMEM_LIMIT),
-    )(own, other)
+    )(left, own, other)
 
 
 def finish_kernel(x_ref, out_ref):
     scale = 1.0 / math.sqrt(R2 * R3 * R4 * R5)
-    factor = jnp.exp2(x_ref[:, 7:8, 64:65])
+    factor = jnp.exp2(x_ref[:, :, PAD - 1:PAD])
     total = jnp.sum(x_ref[...] * factor, axis=0) * scale
-    rows = jnp.concatenate([total[:, :64], total[:, 64:]], axis=0)[:ROWS]
-    group = [rows[:, g * PAD:g * PAD + ROWS] for g in range(4)]
+    place = lax.axis_index("y")
+    turned = total
+    for k in range(1, 4):
+        turned = jnp.where(place == k, pltpu.roll(total, 128 - 32 * k, 1), turned)
+    own = jnp.concatenate([turned[:, :32], turned[:, 64:96]], axis=0)[:ROWS]
+    other = jnp.concatenate([turned[:, 32:64], turned[:, 96:]], axis=0)[:ROWS]
+    group = [half[:, x * PAD:x * PAD + ROWS] for x in range(XL) for half in (own, other)]
     first = lax.axis_index("core") == 0
     out_ref[...] = jnp.where(
         first, jnp.concatenate(group, axis=1), jnp.concatenate([group[g ^ 1] for g in range(4)], axis=1)
@@ -241,8 +284,10 @@
         rows = lax.all_to_all(core, "z", 0, 0, tiled=True)
     with jax.named_scope("core_swap"):
         other = lax.ppermute(rows, "core", [(0, 1), (1, 0)])
+    with jax.named_scope("own_gram"):
+        left, own = own_gram(rows)
     with jax.named_scope("gram"):
-        parts = gram(rows, other)
+        parts = gram(left, own, other)
     with jax.named_scope("gram_exchange"):
         parts = lax.all_to_all(parts.astype(F16), ("z", "x_lo", "x_hi", "y"), 0, 0, tiled=True).astype(F32)
     with jax.named_scope("finish"):

time: 76.2 us -> 76 us (level)
  transfers between devices with their start and end apart: 1 -> 1, of which waited for: 1 -> 1; matrix products, arithmetic and copies ran while one was open for 0% -> 0% of each run, Pallas kernels for 0% -> 1%
where the time goes in v8:
time: 76 us; the launch traced here: 75.8 us
  blocking collectives  65.6 us (86%)
  Pallas kernels  8.88 us (12%)
  waiting for transfers between devices  1.16 us (2%)
    all_to_all x1, blocking collectives, per_device(): rows = lax.all_to_all(core, 'z', 0, 0, tiled=True)  23.1 us
    all_to_all x1, blocking collectives, per_device(): lax.all_to_all(parts.astype(F16), ('z', 'x_lo', 'x_hi', 'y'), 0, 0, tiled...  21.5 us
    all_to_all x1, blocking collectives, per_device(): gathered = lax.all_to_all(reduced, ('x_hi', 'y', 'x_lo'), 0, 0, tiled=True)  21.1 us
    pallas_call x1, Pallas kernels, squeeze(): pl.pallas_call(squeeze_kernel, in_specs=[hbm] * 4, out_shape=pltpu.VMEM((...  5.06 us
  transfers between devices with their start and end apart: 1, of which 1 were waited for; matrix products, arithmetic and copies ran while one was open for 0% of the time, Pallas kernels for 1%

profile of v8, /device:TPU:6, one launch (start us, length us, event | category | flops | bytes accessed | tf_op | source)
XLA Modules:
  0.0 75.8 jit_solution(8427464044836994889)
XLA Ops:
  0.0 0.0 copy-start
  0.0 5.1 %squeeze.1 = bf16[16,224,128]{2,1,0:T(8,128)(2,1)S(1)} custom-call(f32[14,16,4224]{2,1,0:T(8,128)} %t_hbm.1, f32[16,16]{1,0:T(8,128)} %f3_hbm.1, f32[16,33]{1,0:T(8,128)} %bitcast.3, f32[8,8]{1,0:T(8,128)} %f5_hbm.1), custom_call_target="tpu_custom_call" | custom-call | tf_op jit(solution)/shard_map/squeeze/pallas_call | solution.py:124
  5.1 21.1 %all_to_all.15.x_ref = bf16[16,224,128]{2,1,0:T(8,128)(2,1)S(1)} all-to-all(bf16[16,224,128]{2,1,0:T(8,128)(2,1)S(1)} %squeeze.1), channel_id=1, replica_groups=mesh['z'=8,'x_lo'=2,'core'=2,'x_hi'=2,'y'=4] {'x_hi','y','x_lo'}, dimensions={0} | all-to-all | bytes 1835008 | tf_op jit(solution)/shard_map/depth_exchange/all_to_all | solution.py:280
  26.1 0.0 copy-done
  26.1 1.2 %expand.1 = bf16[8,224,128]{2,1,0:T(8,128)(2,1)S(1)} custom-call(bf16[16,224,128]{2,1,0:T(8,128)(2,1)S(1)} %all_to_all.15.x_ref, f32[64,128]{1,0:T(8,128)S(1)} %bitcast.2), custom_call_target="tpu_custom_call" | custom-call | tf_op jit(solution)/shard_map/expand/pallas_call | solution.py:161
  27.4 23.1 %all_to_all.16.own_ref = bf16[8,224,128]{2,1,0:T(8,128)(2,1)S(1)} all-to-all(bf16[8,224,128]{2,1,0:T(8,128)(2,1)S(1)} %expand.1), channel_id=1, replica_groups=mesh['z'=8,'x_lo'=2,'core'=2,'x_hi'=2,'y'=4] {'z'}, dimensions={0} | all-to-all | bytes 917504 | tf_op jit(solution)/shard_map/row_exchange/all_to_all | solution.py:284
  50.4 0.0 collective-permute-start
  50.5 0.6 own_gram.1
  51.1 1.2 %collective-permute-done.other_ref = bf16[8,224,128]{2,1,0:T(8,128)(2,1)S(1)} collective-permute-done((bf16[8,224,128]{2,1,0:T(8,128)(2,1)S(1)}, bf16[8,224,128]{2,1,0:T(8,128)(2,1)S(1)}, u32[]{:S(2)}, u32[]{:S(2)}) %collective-permute-start) | collective-permute-done | bytes 458784 | tf_op jit(solution)/shard_map/core_swap/ppermute | solution.py:286
  52.3 0.9 %gram.1 = f32[128,8,128]{2,1,0:T(8,128)S(1)} custom-call(bf16[4,256,256]{2,1,0:T(8,128)(2,1)S(1)} %get-tuple-element.7.left_ref, f32[256,256]{1,0:T(8,128)S(1)} %get-tuple-element.8.own_ref, bf16[8,224,128]{2,1,0:T(8,128)(2,1)S(1)} %collective-permute-done.other_ref), custom_call_target="tpu_custom_call" | custom-call | tf_op jit(solution)/shard_map/gram/pallas_call | solution.py:244
  53.2 21.5 %all_to_all.17 = f16[128,8,128]{2,1,0:T(8,128)(2,1)S(1)} all-to-all(f16[128,8,128]{2,1,0:T(8,128)(2,1)S(1)} %convert_element_type.6), channel_id=1, replica_groups=mesh['z'=8,'x_lo'=2,'core'=2,'x_hi'=2,'y'=4] {'z','x_lo','x_hi','y'}, dimensions={0} | all-to-all | bytes 524288 | tf_op jit(solution)/shard_map/gram_exchange/all_to_all | solution.py:292
  74.8 1.0 %finish.1 = f32[14,56]{1,0:T(8,128)} custom-call(f32[128,8,128]{2,1,0:T(8,128)S(1)} %convert_element_type.7.x_ref), custom_call_target="tpu_custom_call" | custom-call | tf_op jit(solution)/shard_map/finish/pallas_call | solution.py:269
  (2 shorter events, 0.1 us)
Async XLA Ops:
  0.0 26.1 %copy-start = (f32[128,64]{0,1:T(8,128)S(1)}, f32[128,64]{0,1:T(8,128)}, u32[]{:S(2)}) copy-start(f32[128,64]{0,1:T(8,128)} %param.6) | copy-start | bytes 98308
  50.4 1.8 %collective-permute-start = (bf16[8,224,128]{2,1,0:T(8,128)(2,1)S(1)}, bf16[8,224,128]{2,1,0:T(8,128)(2,1)S(1)}, u32[]{:S(2)}, u32[]{:S(2)}) collective-permute-start(bf16[8,224,128]{2,1,0:T(8,128)(2,1)S(1)} %all_to_all.16.own_ref), channel_id=1, source_target_pairs={{0,8},{8,0},{1,9},{9,1},{2,10},{10,2},{3,11},{11,3},{4,12},{12,4},... | collective-permute-start | bytes 1376264 | tf_op jit(solution)/shard_map/core_swap/ppermute | solution.py:286

commit v9 on v8

--- a/solution.py
+++ b/solution.py
@@ -17,7 +17,10 @@
 PAIR = R4 * R5
 WIDE = DEPTH
 PAD = 16
-SHIFT = 2.0 ** 24
+MAIN = 256
+DEEP = 2 * INNER - MAIN
+SHIFT_BITS = 24.0
+SHIFT = 2.0 ** SHIFT_BITS
 ROWS_STEP = 2
 Z, XL, CORE, XH, Y = 8, 2, 2, 2, 4
 NARROW = XH * Y
@@ -48,8 +51,8 @@
 
 def decode(code):
     wide = code.astype(F32)
-    size = jnp.exp2(jnp.log2(jnp.abs(wide)) * (1.0 / 3.0)) * (1.0 / SHIFT)
-    return jnp.where(wide == 0.0, 0.0, jnp.where(wide < 0.0, -size, size))
+    power = jnp.log2(jnp.maximum(jnp.abs(wide), 1e-38))
+    return wide * jnp.exp2(power * (-2.0 / 3.0) - SHIFT_BITS)
 
 
 def exact_dot(left, right, dims):
@@ -84,8 +87,9 @@
     five = exact_dot(f5_ref[...], spread_five, ((1,), (0,)))
     pair = (four[:, None, :] * five[None, :, :]).reshape(INNER, PAIR)
     high, low = split(pair)
-    main_h[:, :PAIR] = high
-    main_h[:, PAIR:] = low
+    high, low = high.astype(F32), low.astype(F32)
+    main_h[:, :PAIR] = jnp.concatenate([high, high[MAIN:]], axis=0).astype(BF16)
+    main_h[:, PAIR:] = jnp.concatenate([low, jnp.zeros_like(low[MAIN:])], axis=0).astype(BF16)
     size = R3 * DEPTH
     a_row = lax.broadcasted_iota(jnp.int32, (size, I3), 0) // DEPTH
     a_col = lax.broadcasted_iota(jnp.int32, (size, I3), 1)
@@ -107,10 +111,17 @@
             loads[i].wait()
         halves = [split(t_ref[i]) for i in group]
         starts = [a * INNER for a in range(I3)]
-        left_h = jnp.concatenate([h[:, s:s + INNER] for h, _ in halves for s in starts], axis=0)
-        left_l = jnp.concatenate([l[:, s:s + INNER] for _, l in halves for s in starts], axis=0)
+        left_h = jnp.concatenate(
+            [
+                jnp.concatenate([h[:, s:s + INNER], l[:, s + MAIN:s + INNER]], axis=1)
+                for h, l in halves
+                for s in starts
+            ],
+            axis=0,
+        )
+        left_l = jnp.concatenate([l[:, s:s + MAIN] for _, l in halves for s in starts], axis=0)
         both = dot(left_h, main_h[...])
-        stack = both[:, :PAIR] + (both[:, PAIR:] + dot(left_l, main_h[:, :PAIR]))
+        stack = both[:, :PAIR] + (both[:, PAIR:] + dot(left_l, main_h[:MAIN, :PAIR]))
         for n, i in enumerate(group):
             inner_h, inner_l = split(stack[n * size_in:(n + 1) * size_in])
             both = dot(mix_h[...], jnp.concatenate([inner_h, inner_l], axis=1))
@@ -131,7 +142,7 @@
             pltpu.VMEM((I3, R3), F32),
             pltpu.VMEM((R4, I4), F32),
             pltpu.VMEM((I5, R5), F32),
-            pltpu.VMEM((INNER, 2 * PAIR), BF16),
+            pltpu.VMEM((DEEP, 2 * PAIR), BF16),
             pltpu.VMEM((size, size), BF16),
             pltpu.VMEM((size, size), BF16),
             pltpu.SemaphoreType.DMA((ROWS + 3,)),

time: 76 us -> 75.7 us (level)
  no operation moved by 1% of the time
where the time goes in v9:
time: 75.7 us; the launch traced here: 75.6 us
  blocking collectives  65.6 us (87%)
  Pallas kernels  8.63 us (11%)
  waiting for transfers between devices  1.16 us (2%)
    all_to_all x1, blocking collectives, per_device(): rows = lax.all_to_all(core, 'z', 0, 0, tiled=True)  23.1 us
    all_to_all x1, blocking collectives, per_device(): lax.all_to_all(parts.astype(F16), ('z', 'x_lo', 'x_hi', 'y'), 0, 0, tiled...  21.5 us
    all_to_all x1, blocking collectives, per_device(): gathered = lax.all_to_all(reduced, ('x_hi', 'y', 'x_lo'), 0, 0, tiled=True)  21.1 us
    pallas_call x1, Pallas kernels, squeeze(): pl.pallas_call(squeeze_kernel, in_specs=[hbm] * 4, out_shape=pltpu.VMEM((...  4.99 us
  transfers between devices with their start and end apart: 1, of which 1 were waited for; matrix products, arithmetic and copies ran while one was open for 0% of the time, Pallas kernels for 1%

profile of v9, /device:TPU:6, one launch (start us, length us, event | category | flops | bytes accessed | tf_op | source)
XLA Modules:
  0.0 75.6 jit_solution(16173982641264444037)
XLA Ops:
  0.0 0.0 copy-start
  0.0 5.0 %squeeze.1 = bf16[16,224,128]{2,1,0:T(8,128)(2,1)S(1)} custom-call(f32[14,16,4224]{2,1,0:T(8,128)} %t_hbm.1, f32[16,16]{1,0:T(8,128)} %f3_hbm.1, f32[16,33]{1,0:T(8,128)} %bitcast.3, f32[8,8]{1,0:T(8,128)} %f5_hbm.1), custom_call_target="tpu_custom_call" | custom-call | tf_op jit(solution)/shard_map/squeeze/pallas_call | solution.py:135
  5.0 21.1 %all_to_all.15.x_ref = bf16[16,224,128]{2,1,0:T(8,128)(2,1)S(1)} all-to-all(bf16[16,224,128]{2,1,0:T(8,128)(2,1)S(1)} %squeeze.1), channel_id=1, replica_groups=mesh['z'=8,'x_lo'=2,'core'=2,'x_hi'=2,'y'=4] {'x_hi','y','x_lo'}, dimensions={0} | all-to-all | bytes 1835008 | tf_op jit(solution)/shard_map/depth_exchange/all_to_all | solution.py:291
  26.1 0.0 copy-done
  26.1 1.0 %expand.1 = bf16[8,224,128]{2,1,0:T(8,128)(2,1)S(1)} custom-call(bf16[16,224,128]{2,1,0:T(8,128)(2,1)S(1)} %all_to_all.15.x_ref, f32[64,128]{1,0:T(8,128)S(1)} %bitcast.2), custom_call_target="tpu_custom_call" | custom-call | tf_op jit(solution)/shard_map/expand/pallas_call | solution.py:172
  27.1 23.1 %all_to_all.16.own_ref = bf16[8,224,128]{2,1,0:T(8,128)(2,1)S(1)} all-to-all(bf16[8,224,128]{2,1,0:T(8,128)(2,1)S(1)} %expand.1), channel_id=1, replica_groups=mesh['z'=8,'x_lo'=2,'core'=2,'x_hi'=2,'y'=4] {'z'}, dimensions={0} | all-to-all | bytes 917504 | tf_op jit(solution)/shard_map/row_exchange/all_to_all | solution.py:295
  50.2 0.0 collective-permute-start
  50.2 0.6 own_gram.1
  50.9 1.2 %collective-permute-done.other_ref = bf16[8,224,128]{2,1,0:T(8,128)(2,1)S(1)} collective-permute-done((bf16[8,224,128]{2,1,0:T(8,128)(2,1)S(1)}, bf16[8,224,128]{2,1,0:T(8,128)(2,1)S(1)}, u32[]{:S(2)}, u32[]{:S(2)}) %collective-permute-start) | collective-permute-done | bytes 458784 | tf_op jit(solution)/shard_map/core_swap/ppermute | solution.py:297
  52.0 0.9 %gram.1 = f32[128,8,128]{2,1,0:T(8,128)S(1)} custom-call(bf16[4,256,256]{2,1,0:T(8,128)(2,1)S(1)} %get-tuple-element.7.left_ref, f32[256,256]{1,0:T(8,128)S(1)} %get-tuple-element.8.own_ref, bf16[8,224,128]{2,1,0:T(8,128)(2,1)S(1)} %collective-permute-done.other_ref), custom_call_target="tpu_custom_call" | custom-call | tf_op jit(solution)/shard_map/gram/pallas_call | solution.py:255
  53.0 21.5 %all_to_all.17 = f16[128,8,128]{2,1,0:T(8,128)(2,1)S(1)} all-to-all(f16[128,8,128]{2,1,0:T(8,128)(2,1)S(1)} %convert_element_type.6), channel_id=1, replica_groups=mesh['z'=8,'x_lo'=2,'core'=2,'x_hi'=2,'y'=4] {'z','x_lo','x_hi','y'}, dimensions={0} | all-to-all | bytes 524288 | tf_op jit(solution)/shard_map/gram_exchange/all_to_all | solution.py:303
  74.5 1.0 %finish.1 = f32[14,56]{1,0:T(8,128)} custom-call(f32[128,8,128]{2,1,0:T(8,128)S(1)} %convert_element_type.7.x_ref), custom_call_target="tpu_custom_call" | custom-call | tf_op jit(solution)/shard_map/finish/pallas_call | solution.py:280
  (2 shorter events, 0.1 us)
Async XLA Ops:
  0.0 26.1 %copy-start = (f32[128,64]{0,1:T(8,128)S(1)}, f32[128,64]{0,1:T(8,128)}, u32[]{:S(2)}) copy-start(f32[128,64]{0,1:T(8,128)} %param.6) | copy-start | bytes 98308
  50.2 1.8 %collective-permute-start = (bf16[8,224,128]{2,1,0:T(8,128)(2,1)S(1)}, bf16[8,224,128]{2,1,0:T(8,128)(2,1)S(1)}, u32[]{:S(2)}, u32[]{:S(2)}) collective-permute-start(bf16[8,224,128]{2,1,0:T(8,128)(2,1)S(1)} %all_to_all.16.own_ref), channel_id=1, source_target_pairs={{0,8},{8,0},{1,9},{9,1},{2,10},{10,2},{3,11},{11,3},{4,12},{12,4},... | collective-permute-start | bytes 1376264 | tf_op jit(solution)/shard_map/core_swap/ppermute | solution.py:297

commit v10 on v9

--- a/solution.py
+++ b/solution.py
@@ -122,11 +122,17 @@
         left_l = jnp.concatenate([l[:, s:s + MAIN] for _, l in halves for s in starts], axis=0)
         both = dot(left_h, main_h[...])
         stack = both[:, :PAIR] + (both[:, PAIR:] + dot(left_l, main_h[:MAIN, :PAIR]))
+        inner_h, inner_l = split(stack)
+        wide_h, wide_l = (
+            jnp.concatenate([p[n * size_in:(n + 1) * size_in] for n in range(len(group))], axis=1)
+            for p in (inner_h, inner_l)
+        )
+        outer = dot(
+            jnp.concatenate([mix_h[...], mix_l[...], mix_h[...]], axis=1),
+            jnp.concatenate([wide_h, wide_h, wide_l], axis=0),
+        )
         for n, i in enumerate(group):
-            inner_h, inner_l = split(stack[n * size_in:(n + 1) * size_in])
-            both = dot(mix_h[...], jnp.concatenate([inner_h, inner_l], axis=1))
-            outer = both[:, :PAIR] + (both[:, PAIR:] + dot(mix_l[...], inner_h))
-            out_ref[:, i * WIDE:(i + 1) * WIDE] = encode(outer).reshape(FIRST, WIDE, PAIR)
+            out_ref[:, i * WIDE:(i + 1) * WIDE] = encode(outer[:, n * PAIR:(n + 1) * PAIR]).reshape(FIRST, WIDE, PAIR)
 
 
 def squeeze(tensor, f3, f4t, f5):

time: 75.7 us -> 75.6 us (level)
  no operation moved by 1% of the time
where the time goes in v10:
time: 75.6 us; the launch traced here: 75.4 us
  blocking collectives  65.6 us (87%)
  Pallas kernels  8.51 us (11%)
  waiting for transfers between devices  1.16 us (2%)
    all_to_all x1, blocking collectives, per_device(): rows = lax.all_to_all(core, 'z', 0, 0, tiled=True)  23.1 us
    all_to_all x1, blocking collectives, per_device(): lax.all_to_all(parts.astype(F16), ('z', 'x_lo', 'x_hi', 'y'), 0, 0, tiled...  21.5 us
    all_to_all x1, blocking collectives, per_device(): gathered = lax.all_to_all(reduced, ('x_hi', 'y', 'x_lo'), 0, 0, tiled=True)  21.1 us
    pallas_call x1, Pallas kernels, squeeze(): pl.pallas_call(squeeze_kernel, in_specs=[hbm] * 4, out_shape=pltpu.VMEM((...  4.87 us
  transfers between devices with their start and end apart: 1, of which 1 were waited for; matrix products, arithmetic and copies ran while one was open for 0% of the time, Pallas kernels for 1%

profile of v10, /device:TPU:6, one launch (start us, length us, event | category | flops | bytes accessed | tf_op | source)
XLA Modules:
  0.0 75.4 jit_solution(7182598536013489161)
XLA Ops:
  0.0 0.0 copy-start
  0.0 4.9 %squeeze.1 = bf16[16,224,128]{2,1,0:T(8,128)(2,1)S(1)} custom-call(f32[14,16,4224]{2,1,0:T(8,128)} %t_hbm.1, f32[16,16]{1,0:T(8,128)} %f3_hbm.1, f32[16,33]{1,0:T(8,128)} %bitcast.3, f32[8,8]{1,0:T(8,128)} %f5_hbm.1), custom_call_target="tpu_custom_call" | custom-call | tf_op jit(solution)/shard_map/squeeze/pallas_call | solution.py:141
  4.9 21.1 %all_to_all.15.x_ref = bf16[16,224,128]{2,1,0:T(8,128)(2,1)S(1)} all-to-all(bf16[16,224,128]{2,1,0:T(8,128)(2,1)S(1)} %squeeze.1), channel_id=1, replica_groups=mesh['z'=8,'x_lo'=2,'core'=2,'x_hi'=2,'y'=4] {'x_hi','y','x_lo'}, dimensions={0} | all-to-all | bytes 1835008 | tf_op jit(solution)/shard_map/depth_exchange/all_to_all | solution.py:297
  25.9 0.0 copy-done
  25.9 1.0 %expand.1 = bf16[8,224,128]{2,1,0:T(8,128)(2,1)S(1)} custom-call(bf16[16,224,128]{2,1,0:T(8,128)(2,1)S(1)} %all_to_all.15.x_ref, f32[64,128]{1,0:T(8,128)S(1)} %bitcast.2), custom_call_target="tpu_custom_call" | custom-call | tf_op jit(solution)/shard_map/expand/pallas_call | solution.py:178
  27.0 23.1 %all_to_all.16.own_ref = bf16[8,224,128]{2,1,0:T(8,128)(2,1)S(1)} all-to-all(bf16[8,224,128]{2,1,0:T(8,128)(2,1)S(1)} %expand.1), channel_id=1, replica_groups=mesh['z'=8,'x_lo'=2,'core'=2,'x_hi'=2,'y'=4] {'z'}, dimensions={0} | all-to-all | bytes 917504 | tf_op jit(solution)/shard_map/row_exchange/all_to_all | solution.py:301
  50.1 0.0 collective-permute-start
  50.1 0.6 own_gram.1
  50.7 1.2 %collective-permute-done.other_ref = bf16[8,224,128]{2,1,0:T(8,128)(2,1)S(1)} collective-permute-done((bf16[8,224,128]{2,1,0:T(8,128)(2,1)S(1)}, bf16[8,224,128]{2,1,0:T(8,128)(2,1)S(1)}, u32[]{:S(2)}, u32[]{:S(2)}) %collective-permute-start) | collective-permute-done | bytes 458784 | tf_op jit(solution)/shard_map/core_swap/ppermute | solution.py:303
  51.9 0.9 %gram.1 = f32[128,8,128]{2,1,0:T(8,128)S(1)} custom-call(bf16[4,256,256]{2,1,0:T(8,128)(2,1)S(1)} %get-tuple-element.7.left_ref, f32[256,256]{1,0:T(8,128)S(1)} %get-tuple-element.8.own_ref, bf16[8,224,128]{2,1,0:T(8,128)(2,1)S(1)} %collective-permute-done.other_ref), custom_call_target="tpu_custom_call" | custom-call | tf_op jit(solution)/shard_map/gram/pallas_call | solution.py:261
  52.9 21.5 %all_to_all.17 = f16[128,8,128]{2,1,0:T(8,128)(2,1)S(1)} all-to-all(f16[128,8,128]{2,1,0:T(8,128)(2,1)S(1)} %convert_element_type.6), channel_id=1, replica_groups=mesh['z'=8,'x_lo'=2,'core'=2,'x_hi'=2,'y'=4] {'z','x_lo','x_hi','y'}, dimensions={0} | all-to-all | bytes 524288 | tf_op jit(solution)/shard_map/gram_exchange/all_to_all | solution.py:309
  74.4 1.0 %finish.1 = f32[14,56]{1,0:T(8,128)} custom-call(f32[128,8,128]{2,1,0:T(8,128)S(1)} %convert_element_type.7.x_ref), custom_call_target="tpu_custom_call" | custom-call | tf_op jit(solution)/shard_map/finish/pallas_call | solution.py:286
  (2 shorter events, 0.1 us)
Async XLA Ops:
  0.0 25.9 %copy-start = (f32[128,64]{0,1:T(8,128)S(1)}, f32[128,64]{0,1:T(8,128)}, u32[]{:S(2)}) copy-start(f32[128,64]{0,1:T(8,128)} %param.6) | copy-start | bytes 98308
  50.1 1.8 %collective-permute-start = (bf16[8,224,128]{2,1,0:T(8,128)(2,1)S(1)}, bf16[8,224,128]{2,1,0:T(8,128)(2,1)S(1)}, u32[]{:S(2)}, u32[]{:S(2)}) collective-permute-start(bf16[8,224,128]{2,1,0:T(8,128)(2,1)S(1)} %all_to_all.16.own_ref), channel_id=1, source_target_pairs={{0,8},{8,0},{1,9},{9,1},{2,10},{10,2},{3,11},{11,3},{4,12},{12,4},... | collective-permute-start | bytes 1376264 | tf_op jit(solution)/shard_map/core_swap/ppermute | solution.py:303
